TPU v7x, 32 devices: a whole 2x2x4 slice. The times are simulated.
32 devices in a mesh: rep: 16 (over z, x, core), shard: 2 (over y).
Axes of the slice: x: 2, y: 2, z: 4, core: 2. Of those that a mesh axis runs over, the one named last changes fastest.
Arguments:
- latents: bfloat16 [64, 256, 768], P(('rep', 'shard')), may hold values from -3 to 3
- condition: bfloat16 [64, 768], P(('rep', 'shard')), may hold values from -3 to 3
- output_grad: bfloat16 [64, 256, 768], P(('rep', 'shard')), may hold values from -3 to 3
- w_ada: bfloat16 [2, 768, 4608], P(None, 'shard'), may hold values from -0.21875 to 0.21875
- b_ada: bfloat16 [2, 4608], P(None, 'shard'), may hold values from -0.9 to 0.9
- query_key_value_weight: bfloat16 [2, 768, 2304], P(None, 'shard'), may hold values from -0.21875 to 0.21875
- b_qv: bfloat16 [2, 1536], P(None, 'shard'), may hold values from -0.9 to 0.9
- output_matrix_weight: bfloat16 [2, 768, 768], P(None, 'shard'), may hold values from -0.875 to 0.875
- b_proj: bfloat16 [2, 768], P(None, 'shard'), may hold values from -0.9 to 0.9
- first_linear_weight: bfloat16 [2, 768, 3072], P(None, 'shard'), may hold values from -0.21875 to 0.21875
- b_fc1: bfloat16 [2, 3072], P(None, 'shard'), may hold values from -0.9 to 0.9
- second_linear_weight: bfloat16 [2, 3072, 768], P(None, 'shard'), may hold values from -0.109375 to 0.109375
- b_fc2: bfloat16 [2, 768], P(None, 'shard'), may hold values from -0.9 to 0.9
Outputs:
- outputs: bfloat16 [64, 256, 768], P(('rep', 'shard'))
- latents_grad: float32 [64, 256, 768], P(('rep', 'shard'))
- condition_grad: float32 [64, 768], P(('rep', 'shard'))
- g_w_ada: float32 [2, 768, 4608], P(None, 'shard')
- g_b_ada: float32 [2, 4608], P(None, 'shard')
- gradient_query_key_value: float32 [2, 768, 2304], P(None, 'shard')
- g_b_qv: float32 [2, 1536], P(None, 'shard')
- gradient_output_matrix: float32 [2, 768, 768], P(None, 'shard')
- g_b_proj: float32 [2, 768], P(None, 'shard')
- gradient_first_linear: float32 [2, 768, 3072], P(None, 'shard')
- g_b_fc1: float32 [2, 3072], P(None, 'shard')
- gradient_second_linear: float32 [2, 3072, 768], P(None, 'shard')
- g_b_fc2: float32 [2, 768], P(None, 'shard')
All inputs are finite; a program needn't handle non-finite values.
Results may differ from a plain program's by a relative error of at most 0.018.
Values may be sent and summed in bfloat16 or wider, within the bound.
No kernel may reach another device: no remote copies, remote signals or barrier semaphores. Data moves between devices by JAX's collectives and lax.ppermute only.
A program may use at most 256 MiB of HBM per device.

v0:
```python
import jax
import jax.numpy as jnp
from jax import lax
from jax.sharding import PartitionSpec as P

HEADS = 12


eps = 1e-06
highest = lax.Precision.HIGHEST


def normalize(rows):
    centred = rows - jnp.mean(rows, axis=-1, keepdims=True)
    inverse = lax.rsqrt(jnp.mean(centred * centred, axis=-1, keepdims=True) + eps)
    return (centred * inverse, inverse)


def norm_back(upstream, normed, inverse):
    return inverse * (
        upstream
        - jnp.mean(upstream, axis=-1, keepdims=True)
        - normed * jnp.mean(upstream * normed, axis=-1, keepdims=True)
    )


def gelu_tanh(values):
    return jax.nn.gelu(values, approximate=True)


def modulate(silu_low, w_ada, b_ada):
    modulation = jnp.dot(silu_low.astype(jnp.float32), w_ada.astype(jnp.float32), precision=highest)
    return modulation + b_ada.astype(jnp.float32)


def split_mods(modulation):
    return jnp.split(modulation[:, None, :], 6, axis=-1)


def score_block(query_rows, key_rows):
    factor = query_rows.shape[-1] ** (-0.5)
    return (
        jnp.einsum("sqhd,skhd->shqk", query_rows, key_rows, preferred_element_type=jnp.float32)
        * factor
    )


def split_heads(qkv):
    seq_count, length, triple = qkv.shape
    parts = qkv.reshape(seq_count, length, 3, HEADS, triple // (3 * HEADS))
    return (parts[:, :, 0], parts[:, :, 1], parts[:, :, 2])


def forward_layer(stream, mods, params):
    (
        query_key_value_weight,
        b_qv,
        output_matrix_weight,
        b_proj,
        first_linear_weight,
        b_fc1,
        second_linear_weight,
        b_fc2,
    ) = params
    shift_a, scale_a, gate_a, shift_m, scale_m, gate_m = mods
    seq_count, length, features = stream.shape
    normed_a, inverse_a = normalize(stream)
    attention_input = (normed_a * (1.0 + scale_a) + shift_a).astype(jnp.bfloat16)
    qv_bias = b_qv.astype(jnp.float32)
    query_key_value_bias = jnp.concatenate(
        [qv_bias[:features], jnp.zeros((features,), jnp.float32), qv_bias[features:]]
    )
    qkv = (
        jnp.einsum(
            "xny,yp->xnp",
            attention_input,
            query_key_value_weight,
            preferred_element_type=jnp.float32,
        )
        + query_key_value_bias
    ).astype(jnp.bfloat16)
    query_rows, key_rows, value_rows = split_heads(qkv)
    scores = score_block(query_rows, key_rows)
    log_total = jax.nn.logsumexp(scores, axis=-1, keepdims=True)
    attn_probs = jnp.exp(scores - log_total).astype(jnp.bfloat16)
    attention_output = jnp.einsum(
        "shqk,skhd->sqhd", attn_probs, value_rows, preferred_element_type=jnp.float32
    )
    attention_output = attention_output.astype(jnp.bfloat16).reshape(seq_count, length, features)
    branch = jnp.einsum(
        "xny,yp->xnp", attention_output, output_matrix_weight, preferred_element_type=jnp.float32
    ) + b_proj.astype(jnp.float32)
    middle = stream + gate_a * branch
    normed_m, inverse_m = normalize(middle)
    feedforward_input = (normed_m * (1.0 + scale_m) + shift_m).astype(jnp.bfloat16)
    hidden_pre = jnp.einsum(
        "xny,yp->xnp", feedforward_input, first_linear_weight, preferred_element_type=jnp.float32
    ) + b_fc1.astype(jnp.float32)
    hidden_units = gelu_tanh(hidden_pre).astype(jnp.bfloat16)
    output = jnp.einsum(
        "jxm,mt->jxt", hidden_units, second_linear_weight, preferred_element_type=jnp.float32
    ) + b_fc2.astype(jnp.float32)
    result = middle + gate_m * output
    stored = (
        normed_a,
        inverse_a,
        attention_input,
        qkv,
        log_total,
        attention_output,
        branch,
        normed_m,
        inverse_m,
        feedforward_input,
        hidden_pre,
        hidden_units,
        output,
    )
    return (result, stored)


def backward_layer(upstream, mods, params, stored):
    (
        query_key_value_weight,
        b_qv,
        output_matrix_weight,
        b_proj,
        first_linear_weight,
        b_fc1,
        second_linear_weight,
        b_fc2,
    ) = params
    (
        normed_a,
        inverse_a,
        attention_input,
        qkv,
        log_total,
        attention_output,
        branch,
        normed_m,
        inverse_m,
        feedforward_input,
        hidden_pre,
        hidden_units,
        output,
    ) = stored
    shift_a, scale_a, gate_a, shift_m, scale_m, gate_m = mods
    seq_count, length, features = upstream.shape
    output_gradient_rows = (gate_m * upstream).astype(jnp.bfloat16)
    d_gate_m = jnp.sum(upstream * output, axis=1)
    g_b_fc2 = jnp.sum(output_gradient_rows.astype(jnp.float32), axis=(0, 1))
    gradient_second_linear = jnp.einsum(
        "toh,toi->hi", hidden_units, output_gradient_rows, preferred_element_type=jnp.float32
    )
    hidden_gradient = jnp.einsum(
        "nzp,hp->nzh",
        output_gradient_rows,
        second_linear_weight,
        preferred_element_type=jnp.float32,
    )
    gelu_value, gelu_pull = jax.vjp(gelu_tanh, hidden_pre)
    preactivation_gradient = gelu_pull(hidden_gradient)[0].astype(jnp.bfloat16)
    g_b_fc1 = jnp.sum(preactivation_gradient.astype(jnp.float32), axis=(0, 1))
    gradient_first_linear = jnp.einsum(
        "hpa,hpi->ai", feedforward_input, preactivation_gradient, preferred_element_type=jnp.float32
    )
    feedforward_input_gradient = jnp.einsum(
        "vpt,jt->vpj",
        preactivation_gradient,
        first_linear_weight,
        preferred_element_type=jnp.float32,
    )
    d_shift_m = jnp.sum(feedforward_input_gradient, axis=1)
    d_scale_m = jnp.sum(feedforward_input_gradient * normed_m, axis=1)
    grad_mid = upstream + norm_back(
        feedforward_input_gradient * (1.0 + scale_m), normed_m, inverse_m
    )
    residual_branch_gradient = (gate_a * grad_mid).astype(jnp.bfloat16)
    d_gate_a = jnp.sum(grad_mid * branch, axis=1)
    g_b_proj = jnp.sum(residual_branch_gradient.astype(jnp.float32), axis=(0, 1))
    gradient_output_matrix = jnp.einsum(
        "hpa,hpi->ai",
        attention_output,
        residual_branch_gradient,
        preferred_element_type=jnp.float32,
    )
    attention_gradient = jnp.einsum(
        "vpt,jt->vpj",
        residual_branch_gradient,
        output_matrix_weight,
        preferred_element_type=jnp.float32,
    )
    attention_gradient = attention_gradient.astype(jnp.bfloat16).reshape(
        seq_count, length, HEADS, features // HEADS
    )
    query_rows, key_rows, value_rows = split_heads(qkv)
    scores = score_block(query_rows, key_rows)
    attn_exact = jnp.exp(scores - log_total)
    grad_probs = jnp.einsum(
        "sqhd,skhd->shqk", attention_gradient, value_rows, preferred_element_type=jnp.float32
    )
    row_terms = jnp.sum(grad_probs * attn_exact, axis=-1, keepdims=True)
    grad_scores = (attn_exact * (grad_probs - row_terms)).astype(jnp.bfloat16)
    factor = query_rows.shape[-1] ** (-0.5)
    grad_query = (
        jnp.einsum("shqk,skhd->sqhd", grad_scores, key_rows, preferred_element_type=jnp.float32)
        * factor
    )
    grad_key = (
        jnp.einsum("shqk,sqhd->skhd", grad_scores, query_rows, preferred_element_type=jnp.float32)
        * factor
    )
    grad_value = jnp.einsum(
        "shqk,sqhd->skhd",
        attn_exact.astype(jnp.bfloat16),
        attention_gradient,
        preferred_element_type=jnp.float32,
    )
    query_key_value_gradient = jnp.stack([grad_query, grad_key, grad_value], axis=2).astype(
        jnp.bfloat16
    )
    query_key_value_gradient = query_key_value_gradient.reshape(seq_count, length, 3 * features)
    qkv_sums = jnp.sum(query_key_value_gradient.astype(jnp.float32), axis=(0, 1))
    g_b_qv = jnp.concatenate([qkv_sums[:features], qkv_sums[2 * features :]])
    gradient_query_key_value = jnp.einsum(
        "hpa,hpi->ai", attention_input, query_key_value_gradient, preferred_element_type=jnp.float32
    )
    attention_input_gradient = jnp.einsum(
        "vpt,jt->vpj",
        query_key_value_gradient,
        query_key_value_weight,
        preferred_element_type=jnp.float32,
    )
    d_shift_a = jnp.sum(attention_input_gradient, axis=1)
    d_scale_a = jnp.sum(attention_input_gradient * normed_a, axis=1)
    grad_in = grad_mid + norm_back(attention_input_gradient * (1.0 + scale_a), normed_a, inverse_a)
    grad_mod = jnp.concatenate(
        [d_shift_a, d_scale_a, d_gate_a, d_shift_m, d_scale_m, d_gate_m], axis=-1
    )
    grads = (
        gradient_query_key_value,
        g_b_qv,
        gradient_output_matrix,
        g_b_proj,
        gradient_first_linear,
        g_b_fc1,
        gradient_second_linear,
        g_b_fc2,
    )
    return (grad_in, grad_mod, grads)


def local(
    latents,
    condition,
    output_grad,
    w_ada,
    b_ada,
    query_key_value_weight,
    b_qv,
    output_matrix_weight,
    b_proj,
    first_linear_weight,
    b_fc1,
    second_linear_weight,
    b_fc2,
):
    layer_count = w_ada.shape[0]
    cond_value = condition.astype(jnp.float32)
    silu_low = jax.nn.silu(cond_value).astype(jnp.bfloat16)
    stream = latents.astype(jnp.float32)
    gathered_list = []
    mods_list = []
    stored_list = []
    for layer_index in range(layer_count):
        gathered = (
            lax.all_gather(w_ada[layer_index], "shard", axis=0, tiled=True),
            lax.all_gather(b_ada[layer_index], "shard", axis=0, tiled=True),
            lax.all_gather(query_key_value_weight[layer_index], "shard", axis=0, tiled=True),
            lax.all_gather(b_qv[layer_index], "shard", axis=0, tiled=True),
            lax.all_gather(output_matrix_weight[layer_index], "shard", axis=0, tiled=True),
            lax.all_gather(b_proj[layer_index], "shard", axis=0, tiled=True),
            lax.all_gather(first_linear_weight[layer_index], "shard", axis=0, tiled=True),
            lax.all_gather(b_fc1[layer_index], "shard", axis=0, tiled=True),
            lax.all_gather(second_linear_weight[layer_index], "shard", axis=0, tiled=True),
            lax.all_gather(b_fc2[layer_index], "shard", axis=0, tiled=True),
        )
        mods = split_mods(modulate(silu_low, gathered[0], gathered[1]))
        gathered = tuple(gathered)
        stream, stored = forward_layer(stream, mods, gathered[-8:])
        gathered_list.append(gathered)
        mods_list.append(mods)
        stored_list.append(stored)
    outputs = stream.astype(jnp.bfloat16)
    upstream = output_grad.astype(jnp.float32)
    grad_silu = jnp.zeros(cond_value.shape, jnp.float32)
    owned = [None] * layer_count
    for layer_index in reversed(range(layer_count)):
        gathered = tuple(
            (
                lax.all_gather(w_ada[layer_index], "shard", axis=0, tiled=True),
                lax.all_gather(b_ada[layer_index], "shard", axis=0, tiled=True),
                lax.all_gather(query_key_value_weight[layer_index], "shard", axis=0, tiled=True),
                lax.all_gather(b_qv[layer_index], "shard", axis=0, tiled=True),
                lax.all_gather(output_matrix_weight[layer_index], "shard", axis=0, tiled=True),
                lax.all_gather(b_proj[layer_index], "shard", axis=0, tiled=True),
                lax.all_gather(first_linear_weight[layer_index], "shard", axis=0, tiled=True),
                lax.all_gather(b_fc1[layer_index], "shard", axis=0, tiled=True),
                lax.all_gather(second_linear_weight[layer_index], "shard", axis=0, tiled=True),
                lax.all_gather(b_fc2[layer_index], "shard", axis=0, tiled=True),
            )
        )
        upstream, grad_mod, grads = backward_layer(
            upstream, mods_list[layer_index], gathered[-8:], stored_list[layer_index]
        )
        g_w_ada = jnp.dot(silu_low.astype(jnp.float32).T, grad_mod, precision=highest)
        g_b_ada = jnp.sum(grad_mod, axis=0)
        grad_silu = grad_silu + jnp.dot(
            grad_mod, gathered[0].astype(jnp.float32).T, precision=highest
        )
        shares = tuple(
            (
                lax.psum_scatter(
                    g_w_ada.astype(jnp.bfloat16), "shard", scatter_dimension=0, tiled=True
                ).astype(jnp.float32),
                lax.psum_scatter(
                    g_b_ada.astype(jnp.bfloat16), "shard", scatter_dimension=0, tiled=True
                ).astype(jnp.float32),
                lax.psum_scatter(
                    grads[0].astype(jnp.bfloat16), "shard", scatter_dimension=0, tiled=True
                ).astype(jnp.float32),
                lax.psum_scatter(
                    grads[1].astype(jnp.bfloat16), "shard", scatter_dimension=0, tiled=True
                ).astype(jnp.float32),
                lax.psum_scatter(
                    grads[2].astype(jnp.bfloat16), "shard", scatter_dimension=0, tiled=True
                ).astype(jnp.float32),
                lax.psum_scatter(
                    grads[3].astype(jnp.bfloat16), "shard", scatter_dimension=0, tiled=True
                ).astype(jnp.float32),
                lax.psum_scatter(
                    grads[4].astype(jnp.bfloat16), "shard", scatter_dimension=0, tiled=True
                ).astype(jnp.float32),
                lax.psum_scatter(
                    grads[5].astype(jnp.bfloat16), "shard", scatter_dimension=0, tiled=True
                ).astype(jnp.float32),
                lax.psum_scatter(
                    grads[6].astype(jnp.bfloat16), "shard", scatter_dimension=0, tiled=True
                ).astype(jnp.float32),
                lax.psum_scatter(
                    grads[7].astype(jnp.bfloat16), "shard", scatter_dimension=0, tiled=True
                ).astype(jnp.float32),
            )
        )
        owned[layer_index] = shares
    stacked = [
        jnp.stack([owned[layer_index][member] for layer_index in range(layer_count)])
        for member in range(10)
    ]
    stacked = (
        lax.psum(stacked[0].astype(jnp.bfloat16), "rep").astype(jnp.float32),
        lax.psum(stacked[1].astype(jnp.bfloat16), "rep").astype(jnp.float32),
        lax.psum(stacked[2].astype(jnp.bfloat16), "rep").astype(jnp.float32),
        lax.psum(stacked[3].astype(jnp.bfloat16), "rep").astype(jnp.float32),
        lax.psum(stacked[4].astype(jnp.bfloat16), "rep").astype(jnp.float32),
        lax.psum(stacked[5].astype(jnp.bfloat16), "rep").astype(jnp.float32),
        lax.psum(stacked[6].astype(jnp.bfloat16), "rep").astype(jnp.float32),
        lax.psum(stacked[7].astype(jnp.bfloat16), "rep").astype(jnp.float32),
        lax.psum(stacked[8].astype(jnp.bfloat16), "rep").astype(jnp.float32),
        lax.psum(stacked[9].astype(jnp.bfloat16), "rep").astype(jnp.float32),
    )
    silu_value, silu_pull = jax.vjp(jax.nn.silu, cond_value)
    condition_grad = silu_pull(grad_silu)[0]
    return (
        outputs,
        upstream,
        condition_grad,
        stacked[0],
        stacked[1],
        stacked[2],
        stacked[3],
        stacked[4],
        stacked[5],
        stacked[6],
        stacked[7],
        stacked[8],
        stacked[9],
    )


def solution(mesh):
    return jax.shard_map(
        local,
        mesh=mesh,
        in_specs=(
            P(("rep", "shard"), None, None),
            P(("rep", "shard"), None),
            P(("rep", "shard"), None, None),
            P(None, "shard", None),
            P(None, "shard"),
            P(None, "shard", None),
            P(None, "shard"),
            P(None, "shard", None),
            P(None, "shard"),
            P(None, "shard", None),
            P(None, "shard"),
            P(None, "shard", None),
            P(None, "shard"),
        ),
        out_specs=(
            P(("rep", "shard"), None, None),
            P(("rep", "shard"), None, None),
            P(("rep", "shard"), None),
            P(None, "shard", None),
            P(None, "shard"),
            P(None, "shard", None),
            P(None, "shard"),
            P(None, "shard", None),
            P(None, "shard"),
            P(None, "shard", None),
            P(None, "shard"),
            P(None, "shard", None),
            P(None, "shard"),
        ),
        check_vma=False,
    )
```

profile of v0, /device:TPU:1, one launch (start us, length us, event | category | flops | bytes accessed | tf_op | source)
XLA Modules:
  0.0 1633.1 jit_solution(8474110110111672851)
XLA Ops:
  7.2 6.5 fusion.130
  20.2 5.4 fusion.131
  25.6 5.6 fusion.132
  72.6 33.5 %all-gather.31.cloned.1.call-done = bf16[1,768,4608]{2,1,0:T(8,128)(2,1)} async-done(((bf16[1,384,4608]{2,1,0:T(8,128)(2,1)}), bf16[1,768,4608]{2,1,0:T(8,128)(2,1)}) %all-gather.31.cloned.1.call-update) | async-done | bytes 7077904 | tf_op jit(solution)/shard_map/all_gather | solution.py:278
  110.2 47.5 %all-gather.33.cloned.1.call-done = bf16[1,768,2304]{2,1,0:T(8,128)(2,1)} async-done(((bf16[1,384,2304]{2,1,0:T(8,128)(2,1)}), bf16[1,768,2304]{2,1,0:T(8,128)(2,1)}) %all-gather.33.cloned.1.call-update) | async-done | bytes 3538960 | tf_op jit(solution)/shard_map/all_gather | solution.py:280
  157.7 5.6 fusion.50
  171.9 10.7 all-gather.35.cloned.1.call-done
  186.5 60.2 %all-gather.37.cloned.1.call-done = bf16[1,768,3072]{2,1,0:T(8,128)(2,1)} async-done(((bf16[1,384,3072]{2,1,0:T(8,128)(2,1)}), bf16[1,768,3072]{2,1,0:T(8,128)(2,1)}) %all-gather.37.cloned.1.call-update) | async-done | bytes 4718608 | tf_op jit(solution)/shard_map/all_gather | solution.py:284
  246.7 7.1 fusion.48
  253.8 57.5 %all-gather.39.cloned.1.call-done = bf16[1,3072,768]{2,1,0:T(8,128)(2,1)} async-done(((bf16[1,1536,768]{2,1,0:T(8,128)(2,1)}), bf16[1,3072,768]{2,1,0:T(8,128)(2,1)}) %all-gather.39.cloned.1.call-update) | async-done | bytes 4718608 | tf_op jit(solution)/shard_map/all_gather | solution.py:286
  311.3 9.3 fusion.128
  321.0 81.6 %all-gather.41.cloned.1.call-done = bf16[1,768,4608]{2,1,0:T(8,128)(2,1)} async-done(((bf16[1,384,4608]{2,1,0:T(8,128)(2,1)}), bf16[1,768,4608]{2,1,0:T(8,128)(2,1)}) %all-gather.41.cloned.1.call-update) | async-done | bytes 7077904 | tf_op jit(solution)/shard_map/all_gather | solution.py:278
  406.6 46.9 %all-gather.43.cloned.1.call-done = bf16[1,768,2304]{2,1,0:T(8,128)(2,1)} async-done(((bf16[1,384,2304]{2,1,0:T(8,128)(2,1)}), bf16[1,768,2304]{2,1,0:T(8,128)(2,1)}) %all-gather.43.cloned.1.call-update) | async-done | bytes 3538960 | tf_op jit(solution)/shard_map/all_gather | solution.py:280
  453.5 5.5 fusion.51
  466.9 11.6 all-gather.45.cloned.1.call-done
  482.6 60.1 %all-gather.47.cloned.1.call-done = bf16[1,768,3072]{2,1,0:T(8,128)(2,1)} async-done(((bf16[1,384,3072]{2,1,0:T(8,128)(2,1)}), bf16[1,768,3072]{2,1,0:T(8,128)(2,1)}) %all-gather.47.cloned.1.call-update) | async-done | bytes 4718608 | tf_op jit(solution)/shard_map/all_gather | solution.py:284
  542.7 7.4 fusion.40
  550.1 56.7 %all-gather.49.cloned.1.call-done = bf16[1,3072,768]{2,1,0:T(8,128)(2,1)} async-done(((bf16[1,1536,768]{2,1,0:T(8,128)(2,1)}), bf16[1,3072,768]{2,1,0:T(8,128)(2,1)}) %all-gather.49.cloned.1.call-update) | async-done | bytes 4718608 | tf_op jit(solution)/shard_map/all_gather | solution.py:286
  606.8 9.7 fusion.142
  621.8 5.5 fusion.79
  636.9 5.1 convolution_bitcast_fusion.1
  658.3 6.7 fusion.143
  672.9 6.2 bitcast_convert_fusion.4
  685.7 5.2 multiply_reduce_fusion
  704.4 10.3 bitcast_convert_fusion
  714.8 8.9 bitcast_convert_fusion.1
  723.7 7.4 bitcast_convert_fusion.2
  731.8 7.4 bitcast_convert_fusion.3
  739.4 5.4 fusion.76
  747.4 7.8 convolution_convert_fusion.1
  757.9 7.8 convolution_convert_fusion
  768.2 28.3 %reduce-scatter.15.cloned.1.call-done = bf16[384,2304]{1,0:T(8,128)(2,1)} async-done(((bf16[768,2304]{1,0:T(8,128)(2,1)}), bf16[384,2304]{1,0:T(8,128)(2,1)}) %reduce-scatter.15.cloned.1.call-update) | async-done | bytes 1769488 | tf_op jit(solution)/shard_map/reduce_scatter | solution.py:330
  800.6 58.0 %reduce-scatter.29.cloned.1.call-done = bf16[1536,768]{1,0:T(8,128)(2,1)} async-done(((bf16[3072,768]{1,0:T(8,128)(2,1)}), bf16[1536,768]{1,0:T(8,128)(2,1)}) %reduce-scatter.29.cloned.1.call-update) | async-done | bytes 2359312 | tf_op jit(solution)/shard_map/reduce_scatter | solution.py:348
  858.6 62.3 %reduce-scatter.27.cloned.1.call-done = bf16[1536,768]{1,0:T(8,128)(2,1)} async-done(((bf16[3072,768]{1,0:T(8,128)(2,1)}), bf16[1536,768]{1,0:T(8,128)(2,1)}) %reduce-scatter.27.cloned.1.call-update) | async-done | bytes 2359312 | tf_op jit(solution)/shard_map/reduce_scatter | solution.py:348
  920.9 4.9 pad_maximum_fusion.2
  925.8 57.8 %reduce-scatter.25.cloned.1.call-done = bf16[384,3072]{1,0:T(8,128)(2,1)} async-done(((bf16[768,3072]{1,0:T(8,128)(2,1)}), bf16[384,3072]{1,0:T(8,128)(2,1)}) %reduce-scatter.25.cloned.1.call-update) | async-done | bytes 2359312 | tf_op jit(solution)/shard_map/reduce_scatter | solution.py:342
  983.7 62.9 %reduce-scatter.23.cloned.1.call-done = bf16[384,3072]{1,0:T(8,128)(2,1)} async-done(((bf16[768,3072]{1,0:T(8,128)(2,1)}), bf16[384,3072]{1,0:T(8,128)(2,1)}) %reduce-scatter.23.cloned.1.call-update) | async-done | bytes 2359312 | tf_op jit(solution)/shard_map/reduce_scatter | solution.py:342
  1046.5 5.0 pad_maximum_fusion.1
  1051.5 83.5 %reduce-scatter.11.cloned.1.call-done = bf16[384,4608]{1,0:T(8,128)(2,1)} async-done(((bf16[768,4608]{1,0:T(8,128)(2,1)}), bf16[384,4608]{1,0:T(8,128)(2,1)}) %reduce-scatter.11.cloned.1.call-update) | async-done | bytes 3538960 | tf_op jit(solution)/shard_map/reduce_scatter | solution.py:324
  1135.0 88.4 %reduce-scatter.13.cloned.1.call-done = bf16[384,4608]{1,0:T(8,128)(2,1)} async-done(((bf16[768,4608]{1,0:T(8,128)(2,1)}), bf16[384,4608]{1,0:T(8,128)(2,1)}) %reduce-scatter.13.cloned.1.call-update) | async-done | bytes 3538960 | tf_op jit(solution)/shard_map/reduce_scatter | solution.py:324
  1223.5 6.7 pad_maximum_fusion
  1234.5 6.0 all-reduce.12
  1241.5 61.3 %all-reduce.10 = (bf16[2,2304]{1,0:T(2,128)(2,1)S(1)}, bf16[2,768]{1,0:T(2,128)(2,1)S(1)}, bf16[2,384]{1,0:T(2,128)(2,1)S(1)}, bf16[2,1536]{1,0:T(2,128)(2,1)S(1)}, bf16[2,384]{1,0:T(2,128)(2,1)S(1)}) all-reduce(bf16[2,2304]{1,0:T(2,128)(2,1)S(1)} %pad_maximum_fusion.7, ...), channel_id=1, replica_groups=mesh['rep'=16,'shard'=2] {'rep'}, use_global_device_ids=true, to_apply=%region_41.42 | all-reduce | flops 10752 | bytes 43008 | tf_op jit(solution)/shard_map/psum | solution.py:363
  1305.8 8.2 fusion
  1314.0 8.4 fusion.107
  1322.4 276.8 %all-reduce.15.cloned.1.call-done = (bf16[2,384,4608]{2,1,0:T(8,128)(2,1)}, bf16[2,384,2304]{2,1,0:T(8,128)(2,1)}, bf16[2,384,768]{2,1,0:T(8,128)(2,1)}, bf16[2,...) async-done(((bf16[2,384,4608]{2,1,0:T(8,128)(2,1)}, bf16[2,384,2304]{2,1,0:T(8,128)(2,1)}, bf16[2,384,768]{2,1,0:T(8,128)(2,1)}, bf16[2,384,3072]{2,1,0:T(8,128)(2,1)}, ...) | async-done | bytes 21233680 | tf_op jit(solution)/shard_map/psum | solution.py:362
  1602.3 10.4 convert_element_type.306
  1616.4 5.0 convert_element_type.322
  (331 shorter events, 168.8 us)
Async XLA Ops:
  7.2 99.0 %all-gather.31.cloned.1.call-start = ((), (), s32[]{:S(2)}) async-start(), calls=%async_computation.20 | async-start | bytes 10616832 | tf_op jit(solution)/shard_map/all_gather | solution.py:278
  13.7 143.9 %all-gather.33.cloned.1.call-start = ((), (), s32[]{:S(2)}) async-start(), calls=%async_computation.21 | async-start | bytes 5308416 | tf_op jit(solution)/shard_map/all_gather | solution.py:280
  17.8 164.8 %all-gather.35.cloned.1.call-start = ((), (), s32[]{:S(2)}) async-start(), calls=%async_computation.22 | async-start | bytes 1769472 | tf_op jit(solution)/shard_map/all_gather | solution.py:282
  20.2 226.5 %all-gather.37.cloned.1.call-start = ((), (), s32[]{:S(2)}) async-start(), calls=%async_computation.23 | async-start | bytes 7077888 | tf_op jit(solution)/shard_map/all_gather | solution.py:284
  25.6 285.7 %all-gather.39.cloned.1.call-start = ((), (), s32[]{:S(2)}) async-start(), calls=%async_computation.24 | async-start | bytes 7077888 | tf_op jit(solution)/shard_map/all_gather | solution.py:286
  31.2 371.4 %all-gather.41.cloned.1.call-start = ((), (), s32[]{:S(2)}) async-start(), calls=%async_computation.25 | async-start | bytes 10616832 | tf_op jit(solution)/shard_map/all_gather | solution.py:278
  31.8 421.7 %all-gather.43.cloned.1.call-start = ((), (), s32[]{:S(2)}) async-start(), calls=%async_computation.26 | async-start | bytes 5308416 | tf_op jit(solution)/shard_map/all_gather | solution.py:280
  32.6 445.9 %all-gather.45.cloned.1.call-start = ((), (), s32[]{:S(2)}) async-start(), calls=%async_computation.27 | async-start | bytes 1769472 | tf_op jit(solution)/shard_map/all_gather | solution.py:282
  33.3 509.4 %all-gather.47.cloned.1.call-start = ((), (), s32[]{:S(2)}) async-start(), calls=%async_computation.28 | async-start | bytes 7077888 | tf_op jit(solution)/shard_map/all_gather | solution.py:284
  33.4 9.8 copy-start.40
  33.4 16.9 %copy-start.35 = (bf16[2,768]{1,0:T(2,128)(2,1)S(1)}, bf16[2,768]{1,0:T(2,128)(2,1)}, u32[]{:S(2)}) copy-start(bf16[2,768]{1,0:T(2,128)(2,1)} %param.19) | copy-start | bytes 9220
  33.4 24.0 %copy-start.32 = (bf16[2,1536]{1,0:T(2,128)(2,1)S(1)}, bf16[2,1536]{1,0:T(2,128)(2,1)}, u32[]{:S(2)}) copy-start(bf16[2,1536]{1,0:T(2,128)(2,1)} %param.23) | copy-start | bytes 18436
  33.4 31.4 %copy-start.31 = (bf16[2,2304]{1,0:T(2,128)(2,1)S(1)}, bf16[2,2304]{1,0:T(2,128)(2,1)}, u32[]{:S(2)}) copy-start(bf16[2,2304]{1,0:T(2,128)(2,1)} %param.17) | copy-start | bytes 27652
  33.4 72.7 %copy-start.29 = (bf16[2,768]{1,0:T(2,128)(2,1)S(1)}, bf16[2,768]{1,0:T(2,128)(2,1)}, u32[]{:S(2)}) copy-start(bf16[2,768]{1,0:T(2,128)(2,1)} %param.14) | copy-start | bytes 9220
  34.1 572.7 %all-gather.49.cloned.1.call-start = ((), (), s32[]{:S(2)}) async-start(), calls=%async_computation.29 | async-start | bytes 7077888 | tf_op jit(solution)/shard_map/all_gather | solution.py:286
  34.6 731.1 %reduce-scatter.21.cloned.1.call-start = ((), (), s32[]{:S(2)}) async-start(), calls=%async_computation.15 | async-start | bytes 1769472 | tf_op jit(solution)/shard_map/reduce_scatter | solution.py:336
  50.2 261.1 %copy-start.33 = (f32[768]{0:T(1024)}, f32[768]{0:T(1024)S(1)}, u32[]{:S(2)}) copy-start(f32[768]{0:T(1024)S(1)} %convert_reduce_fusion.5) | copy-start | bytes 9220
  110.2 136.5 %copy-start.37 = (f32[2,768]{1,0:T(2,128)}, f32[2,768]{1,0:T(2,128)S(1)}, u32[]{:S(2)}) copy-start(f32[2,768]{1,0:T(2,128)S(1)} %get-tuple-element.98) | copy-start | bytes 18436
  186.1 125.2 %copy-start.4 = (f32[2,256,768]{2,1,0:T(8,128)}, f32[2,256,768]{2,1,0:T(8,128)S(1)}, u32[]{:S(2)}) copy-start(f32[2,256,768]{2,1,0:T(8,128)S(1)} %get-tuple-element.71) | copy-start | bytes 4718596
  320.7 132.9 %copy-start.8 = (f32[2,256,768]{2,1,0:T(8,128)}, f32[2,256,768]{2,1,0:T(8,128)S(1)}, u32[]{:S(2)}) copy-start(f32[2,256,768]{2,1,0:T(8,128)S(1)} %get-tuple-element.69) | copy-start | bytes 4718596
  482.3 145.0 %copy-start.10 = (f32[2,256,768]{2,1,0:T(8,128)}, f32[2,256,768]{2,1,0:T(8,128)S(1)}, u32[]{:S(2)}) copy-start(f32[2,256,768]{2,1,0:T(8,128)S(1)} %get-tuple-element.67) | copy-start | bytes 4718596
  542.7 64.1 %copy-start.25 = (bf16[2,256,768]{2,1,0:T(8,128)(2,1)S(1)}, bf16[2,256,768]{2,1,0:T(8,128)(2,1)}, u32[]{:S(2)}) copy-start(bf16[2,256,768]{2,1,0:T(8,128)(2,1)} %param.15) | copy-start | bytes 2359300
  606.8 9.7 copy-start.41
  616.5 5.3 copy-start.45
  632.2 9.9 slice-start.2
  650.7 115.1 %reduce-scatter.19.cloned.1.call-start = ((), (), s32[]{:S(2)}) async-start(), calls=%async_computation.14 | async-start | bytes 1769472 | tf_op jit(solution)/shard_map/reduce_scatter | solution.py:336
  651.2 6.3 slice-start.10
  651.2 6.3 slice-start.12
  651.5 5.3 copy-start.22
  656.8 8.3 slice-start.8
  657.5 7.5 copy-start.26
  658.3 6.8 copy-start.5
  658.3 6.8 slice-start.9
  672.9 95.3 %reduce-scatter.17.cloned.1.call-start = ((), (), s32[]{:S(2)}) async-start(), calls=%async_computation.13 | async-start | bytes 5308416 | tf_op jit(solution)/shard_map/reduce_scatter | solution.py:330
  679.2 117.3 %reduce-scatter.15.cloned.1.call-start = ((), (), s32[]{:S(2)}) async-start(), calls=%async_computation.12 | async-start | bytes 5308416 | tf_op jit(solution)/shard_map/reduce_scatter | solution.py:330
  704.1 154.5 %reduce-scatter.29.cloned.1.call-start = ((), (), s32[]{:S(2)}) async-start(), calls=%async_computation.19 | async-start | bytes 7077888 | tf_op jit(solution)/shard_map/reduce_scatter | solution.py:348
  714.7 206.2 %reduce-scatter.27.cloned.1.call-start = ((), (), s32[]{:S(2)}) async-start(), calls=%async_computation.18 | async-start | bytes 7077888 | tf_op jit(solution)/shard_map/reduce_scatter | solution.py:348
  723.7 260.0 %reduce-scatter.25.cloned.1.call-start = ((), (), s32[]{:S(2)}) async-start(), calls=%async_computation.17 | async-start | bytes 7077888 | tf_op jit(solution)/shard_map/reduce_scatter | solution.py:342
  731.2 315.4 %reduce-scatter.23.cloned.1.call-start = ((), (), s32[]{:S(2)}) async-start(), calls=%async_computation.16 | async-start | bytes 7077888 | tf_op jit(solution)/shard_map/reduce_scatter | solution.py:342
  739.3 395.7 %reduce-scatter.11.cloned.1.call-start = ((), (), s32[]{:S(2)}) async-start(), calls=%async_computation.10 | async-start | bytes 10616832 | tf_op jit(solution)/shard_map/reduce_scatter | solution.py:324
  739.3 5.5 copy-start.14
  739.3 5.5 copy-start.15
  755.2 468.3 %reduce-scatter.13.cloned.1.call-start = ((), (), s32[]{:S(2)}) async-start(), calls=%async_computation.11 | async-start | bytes 10616832 | tf_op jit(solution)/shard_map/reduce_scatter | solution.py:324
  765.7 833.5 %all-reduce.15.cloned.1.call-start = ((), (), s32[]{:S(2)}) async-start(), calls=%async_computation.30 | async-start | bytes 42467328 | tf_op jit(solution)/shard_map/psum | solution.py:362
  1599.3 17.1 %slice-start.6 = ((s8[4718592]{0:T(1024)(128)(4,1)}), s8[4194304]{0:T(1024)(128)(4,1)S(1)}, s32[]{:S(2)}) async-start(s8[4718592]{0:T(1024)(128)(4,1)} %bitcast.283), calls=%async_computation.37 | async-start | bytes 8388608
  1602.2 10.4 copy-start.18
  1602.3 14.2 slice-start.7
  1612.6 8.8 slice-start.4
  (35 other events, 89.3 us)
Sparse Core Ops, SparseCore 0:
  13.9 92.2 all-gather.30
  108.3 49.3 all-gather.32
  159.8 22.7 all-gather.34
  184.0 62.6 all-gather.36
  248.7 62.6 all-gather.38
  313.3 89.2 all-gather.40
  404.1 49.3 all-gather.42
  455.6 22.7 all-gather.44
  480.0 62.6 all-gather.46
  544.1 62.6 all-gather.48
  650.8 21.7 reduce-scatter.20
  674.8 21.7 reduce-scatter.18
  698.8 47.6 reduce-scatter.16
  748.7 47.6 reduce-scatter.14
  798.6 59.9 reduce-scatter.28
  860.9 59.9 reduce-scatter.26
  923.6 59.9 reduce-scatter.24
  986.5 59.9 reduce-scatter.22
  1049.4 85.5 reduce-scatter.10
  1137.8 85.5 reduce-scatter.12
  1230.3 368.9 all-reduce.14
where the time goes:
time: 1640 us; the launch traced here: 1630 us
  waiting for transfers between devices  1190 us (73%)
  matrix products  200 us (12%)
  blocking collectives  104 us (6%)
  other arithmetic  68.3 us (4%)
  local copies, waits for them, and re-layouts  52.4 us (3%)
  between operations  18.3 us (1%)
    psum x1, waiting for transfers between devices, local(): lax.psum(stacked[0].astype(jnp.bfloat16), 'rep').astype(jnp.float32)  277 us
    reduce_scatter x2, waiting for transfers between devices, local(): lax.psum_scatter(g_w_ada.astype(jnp.bfloat16), 'shard', scatter_dimension...  172 us
    reduce_scatter x2, waiting for transfers between devices, local(): lax.psum_scatter(grads[4].astype(jnp.bfloat16), 'shard', scatter_dimensio...  121 us
    all_gather x2, waiting for transfers between devices, local(): lax.all_gather(first_linear_weight[layer_index], 'shard', axis=0, tiled=T...  120 us
    reduce_scatter x2, waiting for transfers between devices, local(): lax.psum_scatter(grads[6].astype(jnp.bfloat16), 'shard', scatter_dimensio...  120 us
    all_gather x2, waiting for transfers between devices, local(): lax.all_gather(w_ada[layer_index], 'shard', axis=0, tiled=True)  115 us
    all_gather x2, waiting for transfers between devices, local(): lax.all_gather(second_linear_weight[layer_index], 'shard', axis=0, tiled=...  114 us
    all_gather x2, waiting for transfers between devices, local(): lax.all_gather(query_key_value_weight[layer_index], 'shard', axis=0, tile...  94.4 us
  transfers between devices with their start and end apart: 21, of which 18 were waited for; matrix products, arithmetic and copies ran while one was open for 14% of the time, Pallas kernels for 0%

commit v1 on v0

v1 whole, which is shorter than its diff:
```python
import functools

import jax
import jax.numpy as jnp
import numpy as np
from jax import lax
from jax.sharding import Mesh
from jax.sharding import PartitionSpec as P

HEADS = 12
eps = 1e-06
f32 = jnp.float32
bf16 = jnp.bfloat16


def normalize(rows):
    centred = rows - jnp.mean(rows, axis=-1, keepdims=True)
    inverse = lax.rsqrt(jnp.mean(centred * centred, axis=-1, keepdims=True) + eps)
    return (centred * inverse, inverse)


def norm_back(upstream, normed, inverse):
    return inverse * (
        upstream
        - jnp.mean(upstream, axis=-1, keepdims=True)
        - normed * jnp.mean(upstream * normed, axis=-1, keepdims=True)
    )


def gelu_tanh(values):
    return jax.nn.gelu(values, approximate=True)


def mm(a, b):
    return jnp.dot(a, b, preferred_element_type=f32)


def mm_t(a, b):
    return lax.dot_general(a, b, (((1,), (1,)), ((), ())), preferred_element_type=f32)


def t_mm(a, b):
    return lax.dot_general(a, b, (((0,), (0,)), ((), ())), preferred_element_type=f32)


def pick(array, index, axis=0):
    return lax.dynamic_index_in_dim(array, index, axis, keepdims=False)


def after(value, token):
    value, _ = lax.optimization_barrier((value, token))
    return value


SWAP = [(0, 1), (1, 0)]


def swap(value, axis):
    return lax.ppermute(value, axis, SWAP)


class Fast:
    def __init__(self):
        self.far = lax.axis_index("far")
        self.near = lax.axis_index("near")
        self.core = lax.axis_index("core")
        self.shard = lax.axis_index("shard")
        self.left = self.far < 2
        self.is_end = jnp.logical_or(self.far == 0, self.far == 3)

    def fetch_first(self, own):
        quarter = own.shape[0] // 4
        piece = lax.dynamic_slice_in_dim(
            own, (self.near * 2 + self.core) * quarter, quarter, 0
        )
        return piece

    def fetch_rest(self, own, a):
        rows, cols = own.shape
        quarter = rows // 4
        b = swap(a, "near")
        a2 = swap(a, "core")
        b2 = swap(b, "core")
        full = jnp.zeros((2 * rows, cols), own.dtype)
        full = lax.dynamic_update_slice(full, own, (self.shard * rows, 0))
        base = (1 - self.shard) * rows
        for value, near, core in (
            (a, self.near, self.core),
            (b, 1 - self.near, self.core),
            (a2, self.near, 1 - self.core),
            (b2, 1 - self.near, 1 - self.core),
        ):
            full = lax.dynamic_update_slice(full, value, (base + (near * 2 + core) * quarter, 0))
        return full

    def relative(self, stack, step):
        return pick(stack, jnp.where(self.left, step, 3 - step))

    def line_sum(self, stack):
        end, inner, inner2, end2 = [self.relative(stack, step) for step in range(4)]
        a = lax.ppermute(jnp.stack([inner, inner2, end2]), "far", [(0, 1), (3, 2)])
        b = lax.ppermute(
            jnp.stack(
                [
                    (inner2.astype(f32) + a[1].astype(f32)).astype(bf16),
                    (end2.astype(f32) + a[2].astype(f32)).astype(bf16),
                ]
            ),
            "far",
            [(1, 2), (2, 1)],
        )
        c = lax.ppermute(
            (end.astype(f32) + b[1].astype(f32)).astype(bf16), "far", [(1, 0), (2, 3)]
        )
        return jnp.where(
            self.is_end,
            end.astype(f32) + c.astype(f32),
            inner.astype(f32) + a[0].astype(f32) + b[0].astype(f32),
        ).astype(bf16)

    def line_gather(self, own):
        a = lax.ppermute(own, "far", [(0, 1), (3, 2)])
        b = lax.ppermute(jnp.stack([own, a]), "far", [(1, 2), (2, 1)])
        c = lax.ppermute(jnp.concatenate([own[None], b], 0), "far", [(1, 0), (2, 3)])
        end = jnp.where(self.is_end, own, a)
        inner = jnp.where(self.is_end, c[0], own)
        inner2 = jnp.where(self.is_end, c[1], b[0])
        end2 = jnp.where(self.is_end, c[2], b[1])
        return jnp.stack(
            [
                jnp.where(self.left, end, end2),
                jnp.where(self.left, inner, inner2),
                jnp.where(self.left, inner2, inner),
                jnp.where(self.left, end2, end),
            ]
        )

    def pair_sum(self, stack, axis, at):
        me = lax.axis_index(axis)
        got = swap(pick(stack, 1 - me, at), axis)
        return (pick(stack, me, at).astype(f32) + got.astype(f32)).astype(bf16)

    def pair_gather(self, own, axis, at=0):
        got = swap(own, axis)
        me = lax.axis_index(axis)
        return jnp.stack(
            [jnp.where(me == 0, own, got), jnp.where(me == 0, got, own)], axis=at
        )

    def reduce_weight(self, lhs, rhs, order):
        rows, cols = lhs.shape[1], rhs.shape[1]
        half = cols // 2
        theirs = lax.dynamic_slice_in_dim(rhs, (1 - self.core) * half, half, 1)
        mine = lax.dynamic_slice_in_dim(rhs, self.core * half, half, 1)
        got = swap(t_mm(lhs, theirs).astype(bf16), "core")
        part = (t_mm(lhs, mine) + got.astype(f32)).astype(bf16)
        part = part.reshape(2, 2, 4, rows // 16, half)
        if order == "yzx":
            part = self.pair_sum(part, "shard", 0)
            part = jnp.stack([part[:, place] for place in range(4)])
            part = self.line_sum(part)
            part = self.pair_sum(part, "near", 0)
            part = self.pair_gather(part, "near")
            part = self.line_gather(part)
            part = jnp.stack([part[:, 0], part[:, 1]])
        else:
            part = self.pair_sum(part, "near", 1)
            part = self.pair_sum(part, "shard", 0)
            part = self.line_sum(part)
            part = self.line_gather(part)
            part = self.pair_gather(part, "near")
        part = part.reshape(rows // 2, half)
        got = swap(part, "core")
        mine_first = self.core == 0
        return jnp.concatenate(
            [jnp.where(mine_first, part, got), jnp.where(mine_first, got, part)], axis=1
        ).astype(f32)

    def gather_own(self, value):
        got = swap(value, "shard")
        first = self.shard == 0
        return jnp.stack([jnp.where(first, value, got), jnp.where(first, got, value)])

    def gather_every(self, value):
        value = value[None]
        for axis in ("core", "shard", "near"):
            value = jnp.concatenate([value, swap(value, axis)], 0)
        others = [
            lax.ppermute(value, "far", [(i, i ^ step) for i in range(4)]) for step in (1, 2, 3)
        ]
        return jnp.concatenate([value] + others, 0)

    def to_partner_rows(self, part):
        part = part.reshape(2, -1, part.shape[-1])
        got = swap(pick(part, 1 - self.shard), "shard")
        return pick(part, self.shard) + got


class Plain:
    def __init__(self):
        self.shard = lax.axis_index("shard")

    def fetch_first(self, own):
        return None

    def fetch_rest(self, own, a):
        return lax.all_gather(own, "shard", axis=0, tiled=True)

    def reduce_weight(self, lhs, rhs, order):
        grad = t_mm(lhs, rhs).astype(bf16)
        grad = lax.psum_scatter(grad, "shard", scatter_dimension=0, tiled=True)
        return lax.psum(grad, ("far", "near", "core")).astype(f32)

    def gather_own(self, value):
        return lax.all_gather(value, "shard", axis=0)

    def gather_every(self, value):
        return lax.all_gather(value, ("far", "near", "core", "shard"), axis=0)

    def to_partner_rows(self, part):
        return lax.psum_scatter(part, "shard", scatter_dimension=0, tiled=True)


def heads_of(rows, count):
    return rows.reshape(count, -1, HEADS, rows.shape[-1] // HEADS)


def attention_forward(qkv, count):
    width = qkv.shape[1] // 3
    q, k, v = [heads_of(qkv[:, i * width : (i + 1) * width], count) for i in range(3)]
    factor = q.shape[-1] ** (-0.5)
    scores = jnp.einsum("sqhd,skhd->shqk", q, k, preferred_element_type=f32) * factor
    log_total = jax.nn.logsumexp(scores, axis=-1, keepdims=True)
    probs = jnp.exp(scores - log_total).astype(bf16)
    out = jnp.einsum("shqk,skhd->sqhd", probs, v, preferred_element_type=f32)
    return out.astype(bf16).reshape(qkv.shape[0], width), log_total


def attention_backward(qkv, log_total, grad, count):
    width = qkv.shape[1] // 3
    q, k, v = [heads_of(qkv[:, i * width : (i + 1) * width], count) for i in range(3)]
    grad = heads_of(grad, count)
    factor = q.shape[-1] ** (-0.5)
    scores = jnp.einsum("sqhd,skhd->shqk", q, k, preferred_element_type=f32) * factor
    exact = jnp.exp(scores - log_total)
    grad_probs = jnp.einsum("sqhd,skhd->shqk", grad, v, preferred_element_type=f32)
    row_terms = jnp.sum(grad_probs * exact, axis=-1, keepdims=True)
    grad_scores = (exact * (grad_probs - row_terms)).astype(bf16)
    grad_q = jnp.einsum("shqk,skhd->sqhd", grad_scores, k, preferred_element_type=f32) * factor
    grad_k = jnp.einsum("shqk,sqhd->skhd", grad_scores, q, preferred_element_type=f32) * factor
    grad_v = jnp.einsum("shqk,sqhd->skhd", exact.astype(bf16), grad, preferred_element_type=f32)
    flat = [g.astype(bf16).reshape(qkv.shape[0], width) for g in (grad_q, grad_k, grad_v)]
    return jnp.concatenate(flat, axis=1)


def local(
    fast,
    latents,
    condition,
    output_grad,
    w_ada,
    b_ada,
    query_key_value_weight,
    b_qv,
    output_matrix_weight,
    b_proj,
    first_linear_weight,
    b_fc1,
    second_linear_weight,
    b_fc2,
):
    comm = Fast() if fast else Plain()
    layer_count, owned_rows, ada_width = w_ada.shape
    seq_count, length, features = latents.shape
    tokens = seq_count * length
    shard_count = lax.axis_size("shard")

    cond_value = condition.astype(f32)
    silu_low = jax.nn.silu(cond_value).astype(bf16)
    silu_pair = comm.gather_own(silu_low).reshape(shard_count * seq_count, features)
    silu_mine = lax.dynamic_slice_in_dim(silu_pair, comm.shard * owned_rows, owned_rows, 1)
    biases = (b_ada, b_qv, b_proj, b_fc1, b_fc2)
    widths = [b.shape[1] for b in biases]
    bias_all = comm.gather_own(jnp.concatenate(biases, axis=1))
    cuts = np.cumsum(widths)[:-1]
    full_biases = [
        jnp.moveaxis(part, 0, 1).reshape(layer_count, -1).astype(f32)
        for part in jnp.split(bias_all, cuts, axis=2)
    ]
    mod_part = jnp.concatenate([mm(silu_mine, w_ada[l]) for l in range(layer_count)], axis=1)
    mod_both = comm.to_partner_rows(mod_part).reshape(seq_count, layer_count, ada_width)
    mods = []
    for l in range(layer_count):
        mod = mod_both[:, l] + full_biases[0][l]
        mods.append(jnp.split(mod[:, None, :], 6, axis=-1))
    silu_every = comm.gather_every(silu_low).reshape(-1, features)

    owns = []
    for l in range(layer_count):
        for w in (
            query_key_value_weight,
            output_matrix_weight,
            first_linear_weight,
            second_linear_weight,
        ):
            owns.append(w[l])
    weights = []
    firsts = []
    for index, own in enumerate(owns):
        piece = comm.fetch_first(own)
        if piece is not None:
            if index >= 2:
                piece = after(piece, firsts[index - 2])
            piece = swap(piece, "shard")
        firsts.append(piece)
        weights.append(comm.fetch_rest(own, piece))
    layers = [weights[4 * l : 4 * l + 4] for l in range(layer_count)]

    def spread(rows):
        return rows.reshape(seq_count, length, -1)

    def flat(rows):
        return rows.reshape(tokens, -1)

    stream = latents.astype(f32)
    stored = []
    for l in range(layer_count):
        w_qkv, w_out, w_fc1, w_fc2 = layers[l]
        _, bias_qv, bias_proj, bias_fc1, bias_fc2 = [b[l] for b in full_biases]
        shift_a, scale_a, gate_a, shift_m, scale_m, gate_m = mods[l]
        normed_a, inverse_a = normalize(stream)
        attn_in = flat((normed_a * (1.0 + scale_a) + shift_a).astype(bf16))
        bias_qkv = jnp.concatenate(
            [bias_qv[:features], jnp.zeros((features,), f32), bias_qv[features:]]
        )
        qkv = (mm(attn_in, w_qkv) + bias_qkv).astype(bf16)
        attn_out, log_total = attention_forward(qkv, seq_count)
        branch = spread(mm(attn_out, w_out) + bias_proj)
        middle = stream + gate_a * branch
        normed_m, inverse_m = normalize(middle)
        mlp_in = flat((normed_m * (1.0 + scale_m) + shift_m).astype(bf16))
        hidden_pre = mm(mlp_in, w_fc1) + bias_fc1
        hidden = gelu_tanh(hidden_pre).astype(bf16)
        output = spread(mm(hidden, w_fc2) + bias_fc2)
        stream = middle + gate_m * output
        stored.append(
            (
                normed_a, inverse_a, attn_in, qkv, log_total, attn_out, branch,
                normed_m, inverse_m, mlp_in, hidden_pre, hidden, output,
            )
        )
    outputs = stream.astype(bf16)

    dh = output_grad.astype(f32)
    grads = [None] * layer_count
    small = [None] * layer_count
    grad_mods = [None] * layer_count
    for l in reversed(range(layer_count)):
        w_qkv, w_out, w_fc1, w_fc2 = layers[l]
        shift_a, scale_a, gate_a, shift_m, scale_m, gate_m = mods[l]
        (
            normed_a, inverse_a, attn_in, qkv, log_total, attn_out, branch,
            normed_m, inverse_m, mlp_in, hidden_pre, hidden, output,
        ) = stored[l]
        grad_out = flat((gate_m * dh).astype(bf16))
        g_fc2 = comm.reduce_weight(hidden, grad_out, "yzx" if l else "xyz")
        d_gate_m = jnp.sum(dh * output, axis=1)
        g_b_fc2 = jnp.sum(grad_out.astype(f32), axis=0)
        grad_hidden = mm_t(grad_out, w_fc2)
        _, gelu_pull = jax.vjp(gelu_tanh, hidden_pre)
        grad_pre = gelu_pull(grad_hidden)[0].astype(bf16)
        g_fc1 = comm.reduce_weight(mlp_in, grad_pre, "xyz" if l else "yzx")
        g_b_fc1 = jnp.sum(grad_pre.astype(f32), axis=0)
        grad_mlp_in = spread(mm_t(grad_pre, w_fc1))
        d_shift_m = jnp.sum(grad_mlp_in, axis=1)
        d_scale_m = jnp.sum(grad_mlp_in * normed_m, axis=1)
        grad_mid = dh + norm_back(grad_mlp_in * (1.0 + scale_m), normed_m, inverse_m)
        grad_branch = flat((gate_a * grad_mid).astype(bf16))
        d_gate_a = jnp.sum(grad_mid * branch, axis=1)
        g_b_proj = jnp.sum(grad_branch.astype(f32), axis=0)
        g_out = comm.reduce_weight(attn_out, grad_branch, "xyz")
        grad_attn = mm_t(grad_branch, w_out).astype(bf16)
        grad_qkv = attention_backward(qkv, log_total, grad_attn, seq_count)
        qkv_sums = jnp.sum(grad_qkv.astype(f32), axis=0)
        g_b_qv = jnp.concatenate([qkv_sums[:features], qkv_sums[2 * features :]])
        g_qkv = comm.reduce_weight(attn_in, grad_qkv, "yzx")
        grad_attn_in = spread(mm_t(grad_qkv, w_qkv))
        d_shift_a = jnp.sum(grad_attn_in, axis=1)
        d_scale_a = jnp.sum(grad_attn_in * normed_a, axis=1)
        dh = grad_mid + norm_back(grad_attn_in * (1.0 + scale_a), normed_a, inverse_a)
        grad_mod = jnp.concatenate(
            [d_shift_a, d_scale_a, d_gate_a, d_shift_m, d_scale_m, d_gate_m], axis=-1
        ).astype(bf16)
        grad_mods[l] = grad_mod
        grads[l] = (g_qkv, g_out, g_fc1, g_fc2)
        vector = jnp.concatenate(
            [grad_mod.reshape(-1)] + [g.astype(bf16) for g in (g_b_qv, g_b_proj, g_b_fc1, g_b_fc2)]
        )
        small[l] = comm.gather_every(vector.reshape(-1, 128))

    silu_parts = []
    for l in reversed(range(layer_count)):
        pair = comm.gather_own(grad_mods[l]).reshape(shard_count * seq_count, ada_width)
        silu_parts.append(mm_t(pair, w_ada[l]))
    silu_part = functools.reduce(jnp.add, silu_parts)
    if fast:
        by_owner = silu_part.reshape(2, seq_count, owned_rows)
        got = swap(pick(by_owner, 1 - comm.shard), "shard")
        mine = pick(by_owner, comm.shard)
        first = comm.shard == 0
        grad_silu = jnp.concatenate(
            [jnp.where(first, mine, got), jnp.where(first, got, mine)], axis=1
        )
    else:
        by_owner = silu_part.reshape(shard_count, seq_count, owned_rows)
        got = lax.all_to_all(by_owner, "shard", 0, 0)
        grad_silu = jnp.moveaxis(got, 0, 1).reshape(seq_count, features)
    _, silu_pull = jax.vjp(jax.nn.silu, cond_value)
    condition_grad = silu_pull(grad_silu)[0]

    silu_owned = lax.dynamic_slice_in_dim(silu_every, comm.shard * owned_rows, owned_rows, 1)
    g_w_ada, g_biases = [], []
    for l in range(layer_count):
        devices = small[l].shape[0]
        every_vector = small[l].reshape(devices, -1)
        mod_every = every_vector[:, : seq_count * ada_width].reshape(-1, ada_width)
        g_w_ada.append(t_mm(silu_owned, mod_every))
        sums = [jnp.sum(mod_every.astype(f32), axis=0)]
        rest = jnp.sum(every_vector[:, seq_count * ada_width :].astype(f32), axis=0)
        at = 0
        for width in widths[1:]:
            sums.append(rest[at : at + width * shard_count])
            at += width * shard_count
        g_biases.append(
            [
                lax.dynamic_slice_in_dim(total, comm.shard * width, width, 0)
                for total, width in zip(sums, widths)
            ]
        )
    bias_out = [jnp.stack([g[m] for g in g_biases]) for m in range(5)]
    weight_out = [jnp.stack([g[m] for g in grads]) for m in range(4)]
    return (
        outputs,
        dh,
        condition_grad,
        jnp.stack(g_w_ada),
        bias_out[0],
        weight_out[0],
        bias_out[1],
        weight_out[1],
        bias_out[2],
        weight_out[2],
        bias_out[3],
        weight_out[3],
        bias_out[4],
    )


def solution(mesh):
    rep, shard = mesh.shape["rep"], mesh.shape["shard"]
    core = 2 if rep % 2 == 0 else 1
    near = 2 if rep == 16 else 1
    far = rep // (core * near)
    fast = (far, near, core, shard) == (4, 2, 2, 2)
    fine = Mesh(
        np.asarray(mesh.devices).reshape(far, near, core, shard),
        ("far", "near", "core", "shard"),
    )
    every = ("far", "near", "core", "shard")
    row, row3 = P(every, None), P(every, None, None)
    bias, weight = P(None, "shard"), P(None, "shard", None)
    return jax.shard_map(
        functools.partial(local, fast),
        mesh=fine,
        in_specs=(
            row3, row, row3, weight, bias, weight, bias, weight, bias, weight, bias, weight, bias,
        ),
        out_specs=(
            row3, row3, row, weight, bias, weight, bias, weight, bias, weight, bias, weight, bias,
        ),
        check_vma=False,
    )
```

time: 1640 us -> 995 us (0.61)
  waiting for transfers between devices: 1190 us -> 314 us
  starting transfers between devices: 1.9 us -> 238 us
  local copies, waits for them, and re-layouts: 52.4 us -> 185 us
  blocking collectives: 104 us -> 0 us
  matrix products: 200 us -> 164 us
    all_gather x10 -> x0, waiting for transfers between devices: 466 us -> none  [the longest x2 120 us: local(): lax.all_gather(first_linear_weight[layer_index], 'shard', axis=0, tiled=T...]
    reduce_scatter x10 -> x0, waiting for transfers between devices: 441 us -> none  [the longest x2 172 us: local(): lax.psum_scatter(g_w_ada.astype(jnp.bfloat16), 'shard', scatter_dimension...]
    ppermute x0 -> x144, waiting for transfers between devices: none -> 314 us  [the longest x87 109 us: swap(): return lax.ppermute(value, axis, SWAP)]
    psum x1 -> x0, waiting for transfers between devices: 277 us -> none  [local(): lax.psum(stacked[0].astype(jnp.bfloat16), 'rep').astype(jnp.float32)]
    ppermute x0 -> x144, starting transfers between devices: none -> 238 us  [the longest x87 150 us: swap(): return lax.ppermute(value, axis, SWAP)]
    psum x1 -> x0, blocking collectives: 61.3 us -> none  [local(): lax.psum(stacked[1].astype(jnp.bfloat16), 'rep').astype(jnp.float32)]
    dynamic_update_slice x0 -> x40, local copies, waits for them, and re-layouts: none -> 41.1 us  [the longest x32 32.2 us: fetch_rest(): lax.dynamic_update_slice(full, value, (base + (near * 2 + core) * quarter...]
    all_gather x10 -> x0, blocking collectives: 36.9 us -> none  [the longest x2 7.83 us: local(): lax.all_gather(b_proj[layer_index], 'shard', axis=0, tiled=True)]
  transfers between devices with their start and end apart: 21 -> 144, of which waited for: 18 -> 52; matrix products, arithmetic and copies ran while one was open for 14% -> 33% of each run, Pallas kernels for 0% -> 0%
where the time goes in v1:
time: 995 us; the launch traced here: 983 us
  waiting for transfers between devices  314 us (32%)
  starting transfers between devices  238 us (24%)
  local copies, waits for them, and re-layouts  185 us (19%)
  matrix products  164 us (16%)
  other arithmetic  77.5 us (8%)
    ppermute x87, starting transfers between devices, swap(): return lax.ppermute(value, axis, SWAP)  150 us
    ppermute x87, waiting for transfers between devices, swap(): return lax.ppermute(value, axis, SWAP)  109 us
    ppermute x8, waiting for transfers between devices, line_sum(): lax.ppermute((end.astype(f32) + b[1].astype(f32)).astype(bf16), 'far', [(...  107 us
    dot_general x18, matrix products, t_mm(): lax.dot_general(a, b, (((0,), (0,)), ((), ())), preferred_element_type=f32)  49 us
    dot_general x10, matrix products, mm_t(): lax.dot_general(a, b, (((1,), (1,)), ((), ())), preferred_element_type=f32)  43.8 us
    dot_general x10, matrix products, mm(): return jnp.dot(a, b, preferred_element_type=f32)  39.5 us
    unnamed x329, local copies, waits for them, and re-layouts  38.3 us
    dynamic_update_slice x32, local copies, waits for them, and re-layouts, fetch_rest(): lax.dynamic_update_slice(full, value, (base + (near * 2 + core) * quarter...  32.2 us
  transfers between devices with their start and end apart: 144, of which 52 were waited for; matrix products, arithmetic and copies ran while one was open for 33% of the time, Pallas kernels for 0%

profile of v1, /device:TPU:1, one launch (start us, length us, event | category | flops | bytes accessed | tf_op | source)
XLA Modules:
  0.0 982.8 jit_solution(17508317449483868554)
XLA Ops:
  98.3 10.3 %collective-permute-start.17 = (bf16[384,768]{1,0:T(8,128)(2,1)}, bf16[384,768]{1,0:T(8,128)(2,1)}, u32[]{:S(2)}, u32[]{:S(2)}) collective-permute-start(bf16[384,768]{1,0:T(8,128)(2,1)} %collective-permute-done.15), channel_id=1, source_target_pairs={{0,2},{2,0},{1,3},{3,1},{4,6},{6,4},{5,7},{7,5},{8,10},{10,8},{9,1... | collective-permute-start | bytes 1769480 | tf_op jit(solution)/shard_map/ppermute | solution.py:59
  113.0 5.1 collective-permute-start.25
  119.1 9.4 collective-permute-done.24
  166.5 6.2 collective-permute-done.12
  176.9 7.2 collective-permute-done.20
  187.8 9.8 %collective-permute-done.32 = bf16[384,768]{1,0:T(8,128)(2,1)} collective-permute-done((bf16[384,768]{1,0:T(8,128)(2,1)}, bf16[384,768]{1,0:T(8,128)(2,1)}, u32[]{:S(2)}, u32[]{:S(2)}) %collective-permute-start.32) | collective-permute-done | bytes 589856 | tf_op jit(solution)/shard_map/ppermute | solution.py:59
  206.2 8.4 multiply_convert_fusion.3
  214.6 6.1 convolution_add_fusion.5
  259.3 7.8 multiply_convert_fusion.2
  267.1 8.2 fusion.261
  275.4 7.3 fusion.56
  282.8 6.2 fusion.51
  304.6 5.3 fusion.75
  309.9 7.3 multiply_reduce_fusion.1
  338.1 9.2 fusion.255
  347.3 6.3 fusion.53
  370.1 5.1 fusion.76
  375.2 5.0 multiply_reduce_fusion
  434.9 5.1 collective-permute-start.89
  440.0 19.6 %collective-permute-done.54 = bf16[8,120,128]{2,1,0:T(8,128)(2,1)S(1)} collective-permute-done((bf16[8,120,128]{2,1,0:T(8,128)(2,1)S(1)}, bf16[8,120,128]{2,1,0:T(8,128)(2,1)S(1)}, u32[]{:S(2)}, u32[]{:S(2)}) %collective-permute-start.54) | collective-permute-done | bytes 245792 | tf_op jit(solution)/shard_map/ppermute | solution.py:189
  462.7 5.8 concatenate.294
  477.6 5.7 concatenate.282
  493.0 5.2 convolution_bitcast_fusion.1
  503.4 11.3 %pad_maximum_fusion = f32[2,384,4608]{2,1,0:T(8,128)} fusion(f32[1,384,4608]{2,1,0:T(8,128)} %convolution_bitcast_fusion, f32[1,384,4608]{2,1,0:T(8,128)} %convolution_bitcast_fusion.1), kind=kLoop, calls=%fused_computation | loop fusion | flops 3538944 | bytes 28311552 | tf_op jit(solution)/shard_map/stack | solution.py:446
  522.1 5.1 collective-permute-done.90
  528.6 5.7 collective-permute-done.79
  556.0 12.2 %collective-permute-done.94 = bf16[48,384]{1,0:T(8,128)(2,1)S(1)} collective-permute-done((bf16[48,384]{1,0:T(8,128)(2,1)S(1)}, bf16[48,384]{1,0:T(8,128)(2,1)S(1)}, u32[]{:S(2)}, u32[]{:S(2)}) %collective-permute-start.94) | collective-permute-done | bytes 36896 | tf_op jit(solution)/shard_map/ppermute | solution.py:112
  583.0 12.6 %collective-permute-done.97 = bf16[3,48,384]{2,1,0:T(8,128)(2,1)S(1)} collective-permute-done((bf16[3,48,384]{2,1,0:T(8,128)(2,1)S(1)}, bf16[3,48,384]{2,1,0:T(8,128)(2,1)S(1)}, u32[]{:S(2)}, u32[]{:S(2)}) %collective-permute-start.97) | collective-permute-done | bytes 110624 | tf_op jit(solution)/shard_map/ppermute | solution.py:124
  609.1 19.2 %collective-permute-start.100 = (bf16[768,1536]{1,0:T(8,128)(2,1)S(1)}, bf16[768,1536]{1,0:T(8,128)(2,1)S(1)}, u32[]{:S(2)}, u32[]{:S(2)}) collective-permute-start(bf16[768,1536]{1,0:T(8,128)(2,1)S(1)} %copy-done.120), channel_id=1, source_target_pairs={{0,2},{2,0},{1,3},{3,1},{4,6},{6,4},{5,7},{7,5},{8,10},{10,8},{9,1... | collective-permute-start | bytes 7077896 | tf_op jit(solution)/shard_map/ppermute | solution.py:59
  658.0 17.0 %collective-permute-done.57 = bf16[2,4,48,1152]{3,2,1,0:T(8,128)(2,1)S(1)} collective-permute-done((bf16[2,4,48,1152]{3,2,1,0:T(8,128)(2,1)S(1)}, bf16[2,4,48,1152]{3,2,1,0:T(8,128)(2,1)S(1)}, u32[]{:S(2)}, u32[]{:S(2)}) %collective-permute-start.57) | collective-permute-done | bytes 884768 | tf_op jit(solution)/shard_map/ppermute | solution.py:59
  677.2 11.2 %collective-permute-done.69 = bf16[3,2,48,1152]{3,2,1,0:T(8,128)(2,1)S(1)} collective-permute-done((bf16[3,2,48,1152]{3,2,1,0:T(8,128)(2,1)S(1)}, bf16[3,2,48,1152]{3,2,1,0:T(8,128)(2,1)S(1)}, u32[]{:S(2)}, u32[]{:S(2)}) %collective-permute-start.69) | collective-permute-done | bytes 663584 | tf_op jit(solution)/shard_map/ppermute | solution.py:101
  692.7 10.8 %collective-permute-done.58 = bf16[3,2,48,1152]{3,2,1,0:T(8,128)(2,1)S(1)} collective-permute-done((bf16[3,2,48,1152]{3,2,1,0:T(8,128)(2,1)S(1)}, bf16[3,2,48,1152]{3,2,1,0:T(8,128)(2,1)S(1)}, u32[]{:S(2)}, u32[]{:S(2)}) %collective-permute-start.58) | collective-permute-done | bytes 663584 | tf_op jit(solution)/shard_map/ppermute | solution.py:101
  706.1 8.1 collective-permute-start.135
  714.5 11.1 %collective-permute-done.101 = bf16[2,4,48,1536]{3,2,1,0:T(8,128)(2,1)S(1)} collective-permute-done((bf16[2,4,48,1536]{3,2,1,0:T(8,128)(2,1)S(1)}, bf16[2,4,48,1536]{3,2,1,0:T(8,128)(2,1)S(1)}, u32[]{:S(2)}, u32[]{:S(2)}) %collective-permute-start.101) | collective-permute-done | bytes 1179680 | tf_op jit(solution)/shard_map/ppermute | solution.py:59
  731.2 5.6 collective-permute-done.71
  738.3 5.5 collective-permute-done.60
  759.9 12.5 %collective-permute-done.74 = bf16[2,48,1152]{2,1,0:T(8,128)(2,1)S(1)} collective-permute-done((bf16[2,48,1152]{2,1,0:T(8,128)(2,1)S(1)}, bf16[2,48,1152]{2,1,0:T(8,128)(2,1)S(1)}, u32[]{:S(2)}, u32[]{:S(2)}) %collective-permute-start.74) | collective-permute-done | bytes 221216 | tf_op jit(solution)/shard_map/ppermute | solution.py:122
  776.6 5.2 collective-permute-done.63
  791.0 45.1 %collective-permute-done.116 = bf16[48,1536]{1,0:T(8,128)(2,1)S(1)} collective-permute-done((bf16[48,1536]{1,0:T(8,128)(2,1)S(1)}, bf16[48,1536]{1,0:T(8,128)(2,1)S(1)}, u32[]{:S(2)}, u32[]{:S(2)}) %collective-permute-start.116) | collective-permute-done | bytes 147488 | tf_op jit(solution)/shard_map/ppermute | solution.py:112
  837.4 16.0 %collective-permute-done.127 = bf16[192,384]{1,0:T(8,128)(2,1)S(1)} collective-permute-done((bf16[192,384]{1,0:T(8,128)(2,1)S(1)}, bf16[192,384]{1,0:T(8,128)(2,1)S(1)}, u32[]{:S(2)}, u32[]{:S(2)}) %collective-permute-start.127) | collective-permute-done | bytes 147488 | tf_op jit(solution)/shard_map/ppermute | solution.py:112
  860.0 14.1 %collective-permute-done.137 = bf16[2,192,384]{2,1,0:T(8,128)(2,1)S(1)} collective-permute-done((bf16[2,192,384]{2,1,0:T(8,128)(2,1)S(1)}, bf16[2,192,384]{2,1,0:T(8,128)(2,1)S(1)}, u32[]{:S(2)}, u32[]{:S(2)}) %collective-permute-start.137) | collective-permute-done | bytes 294944 | tf_op jit(solution)/shard_map/ppermute | solution.py:112
  874.9 5.4 collective-permute-done.104
  888.3 13.4 %collective-permute-start.77 = (bf16[384,1152]{1,0:T(8,128)(2,1)S(1)}, bf16[384,1152]{1,0:T(8,128)(2,1)S(1)}, u32[]{:S(2)}, u32[]{:S(2)}) collective-permute-start(bf16[384,1152]{1,0:T(8,128)(2,1)S(1)} %bitcast.912), channel_id=1, source_target_pairs={{0,2},{2,0},{1,3},{3,1},{4,6},{6,4},{5,7},{7,5},{8,10},{10,8},{9,1... | collective-permute-start | bytes 2654216 | tf_op jit(solution)/shard_map/ppermute | solution.py:59
  908.7 4.7 collective-permute-done.140
  933.2 8.1 collective-permute-start.121
  950.9 9.6 collective-permute-start.143
  960.5 5.1 collective-permute-done.109
  966.1 6.8 collective-permute-start.110
  (1030 shorter events, 524.9 us)
Async XLA Ops:
  4.1 64.2 %collective-permute-start.2 = (bf16[2,5376]{1,0:T(2,128)(2,1)S(1)}, bf16[2,5376]{1,0:T(2,128)(2,1)S(1)}, u32[]{:S(2)}, u32[]{:S(2)}) collective-permute-start(bf16[2,5376]{1,0:T(2,128)(2,1)S(1)} %constant_dynamic-update-slice_fusion), channel_id=1, source_target_pairs={{0,1},{1,0},{2,3},{3,2},{4,5},{5,4},{6,7},{7,6},{8,9},{9,8},{10,11... | collective-permute-start | bytes 64520 | tf_op jit(solution)/shard_map/ppermute | solution.py:59
  6.9 52.2 %collective-permute-start = (bf16[2,768]{1,0:T(2,128)(2,1)S(1)}, bf16[2,768]{1,0:T(2,128)(2,1)S(1)}, u32[]{:S(2)}, u32[]{:S(2)}) collective-permute-start(bf16[2,768]{1,0:T(2,128)(2,1)S(1)} %get-tuple-element.56), channel_id=1, source_target_pairs={{0,1},{1,0},{2,3},{3,2},{4,5},{5,4},{6,7},{7,6},{8,9},{9,8},{10,11... | collective-permute-start | bytes 9224 | tf_op jit(solution)/shard_map/ppermute | solution.py:59
  7.0 57.3 %collective-permute-start.38 = (bf16[1,2,768]{2,1,0:T(2,128)(2,1)S(1)}, bf16[1,2,768]{2,1,0:T(2,128)(2,1)S(1)}, u32[]{:S(2)}, u32[]{:S(2)}) collective-permute-start(bf16[1,2,768]{2,1,0:T(2,128)(2,1)S(1)} %bitcast.1016), channel_id=1, source_target_pairs={{0,2},{2,0},{1,3},{3,1},{4,6},{6,4},{5,7},{7,5},{8,10},{10,8},{9,1... | collective-permute-start | bytes 9224 | tf_op jit(solution)/shard_map/ppermute | solution.py:59
  10.8 72.6 %collective-permute-start.7 = (bf16[96,768]{1,0:T(8,128)(2,1)}, bf16[96,768]{1,0:T(8,128)(2,1)}, u32[]{:S(2)}, u32[]{:S(2)}) collective-permute-start(bf16[96,768]{1,0:T(8,128)(2,1)} %dynamic-slice_bitcast_fusion.20), channel_id=1, source_target_pairs={{0,1},{1,0},{2,3},{3,2},{4,5},{5,4},{6,7},{7,6},{8,9},{9,8},{10,11... | collective-permute-start | bytes 442376 | tf_op jit(solution)/shard_map/ppermute | solution.py:59
  16.7 76.4 %collective-permute-start.3 = (bf16[96,2304]{1,0:T(8,128)(2,1)}, bf16[96,2304]{1,0:T(8,128)(2,1)}, u32[]{:S(2)}, u32[]{:S(2)}) collective-permute-start(bf16[96,2304]{1,0:T(8,128)(2,1)} %dynamic-slice_bitcast_fusion.12), channel_id=1, source_target_pairs={{0,1},{1,0},{2,3},{3,2},{4,5},{5,4},{6,7},{7,6},{8,9},{9,8},{10,11... | collective-permute-start | bytes 1327112 | tf_op jit(solution)/shard_map/ppermute | solution.py:59
  93.2 38.5 %collective-permute-start.11 = (bf16[96,3072]{1,0:T(8,128)(2,1)S(1)}, bf16[96,3072]{1,0:T(8,128)(2,1)}, u32[]{:S(2)}, u32[]{:S(2)}) collective-permute-start(bf16[96,3072]{1,0:T(8,128)(2,1)S(1)} %copy-done.87), channel_id=1, source_target_pairs={{0,1},{1,0},{2,3},{3,2},{4,5},{5,4},{6,7},{7,6},{8,9},{9,8},{10,11... | collective-permute-start | bytes 1769480 | tf_op jit(solution)/shard_map/ppermute | solution.py:59
  98.3 62.1 %collective-permute-start.17 = (bf16[384,768]{1,0:T(8,128)(2,1)}, bf16[384,768]{1,0:T(8,128)(2,1)}, u32[]{:S(2)}, u32[]{:S(2)}) collective-permute-start(bf16[384,768]{1,0:T(8,128)(2,1)} %collective-permute-done.15), channel_id=1, source_target_pairs={{0,2},{2,0},{1,3},{3,1},{4,6},{6,4},{5,7},{7,5},{8,10},{10,8},{9,1... | collective-permute-start | bytes 1769480 | tf_op jit(solution)/shard_map/ppermute | solution.py:59
  110.6 46.9 %collective-permute-start.16 = (bf16[384,768]{1,0:T(8,128)(2,1)}, bf16[384,768]{1,0:T(8,128)(2,1)}, u32[]{:S(2)}, u32[]{:S(2)}) collective-permute-start(bf16[384,768]{1,0:T(8,128)(2,1)} %collective-permute-done.15), channel_id=1, source_target_pairs={{0,4},{4,0},{1,5},{5,1},{2,6},{6,2},{3,7},{7,3},{8,12},{12,8},{9,1... | collective-permute-start | bytes 1769480 | tf_op jit(solution)/shard_map/ppermute | solution.py:59
  128.5 35.4 %collective-permute-start.31 = (bf16[384,768]{1,0:T(8,128)(2,1)}, bf16[384,768]{1,0:T(8,128)(2,1)}, u32[]{:S(2)}, u32[]{:S(2)}) collective-permute-start(bf16[384,768]{1,0:T(8,128)(2,1)} %dynamic-slice_bitcast_fusion.7), channel_id=1, source_target_pairs={{0,1},{1,0},{2,3},{3,2},{4,5},{5,4},{6,7},{7,6},{8,9},{9,8},{10,11... | collective-permute-start | bytes 1769480 | tf_op jit(solution)/shard_map/ppermute | solution.py:59
  133.6 28.8 %collective-permute-start.19 = (bf16[96,2304]{1,0:T(8,128)(2,1)}, bf16[96,2304]{1,0:T(8,128)(2,1)}, u32[]{:S(2)}, u32[]{:S(2)}) collective-permute-start(bf16[96,2304]{1,0:T(8,128)(2,1)} %dynamic-slice_bitcast_fusion.11), channel_id=1, source_target_pairs={{0,1},{1,0},{2,3},{3,2},{4,5},{5,4},{6,7},{7,6},{8,9},{9,8},{10,11... | collective-permute-start | bytes 1327112 | tf_op jit(solution)/shard_map/ppermute | solution.py:59
  135.4 38.5 %collective-permute-start.13 = (bf16[96,3072]{1,0:T(8,128)(2,1)}, bf16[96,3072]{1,0:T(8,128)(2,1)}, u32[]{:S(2)}, u32[]{:S(2)}) collective-permute-start(bf16[96,3072]{1,0:T(8,128)(2,1)} %collective-permute-done.11), channel_id=1, source_target_pairs={{0,2},{2,0},{1,3},{3,1},{4,6},{6,4},{5,7},{7,5},{8,10},{10,8},{9,1... | collective-permute-start | bytes 1769480 | tf_op jit(solution)/shard_map/ppermute | solution.py:59
  187.1 35.4 %collective-permute-start.22 = (bf16[96,2304]{1,0:T(8,128)(2,1)S(1)}, bf16[96,2304]{1,0:T(8,128)(2,1)S(1)}, u32[]{:S(2)}, u32[]{:S(2)}) collective-permute-start(bf16[96,2304]{1,0:T(8,128)(2,1)S(1)} %collective-permute-done.20), channel_id=1, source_target_pairs={{0,2},{2,0},{1,3},{3,1},{4,6},{6,4},{5,7},{7,5},{8,10},{10,8},{9,1... | collective-permute-start | bytes 1327112 | tf_op jit(solution)/shard_map/ppermute | solution.py:59
  187.2 69.3 %collective-permute-start.29 = (bf16[96,3072]{1,0:T(8,128)(2,1)}, bf16[96,3072]{1,0:T(8,128)(2,1)}, u32[]{:S(2)}, u32[]{:S(2)}) collective-permute-start(bf16[96,3072]{1,0:T(8,128)(2,1)} %collective-permute-done.27), channel_id=1, source_target_pairs={{0,2},{2,0},{1,3},{3,1},{4,6},{6,4},{5,7},{7,5},{8,10},{10,8},{9,1... | collective-permute-start | bytes 1769480 | tf_op jit(solution)/shard_map/ppermute | solution.py:59
  197.6 54.8 %collective-permute-start.28 = (bf16[96,3072]{1,0:T(8,128)(2,1)}, bf16[96,3072]{1,0:T(8,128)(2,1)}, u32[]{:S(2)}, u32[]{:S(2)}) collective-permute-start(bf16[96,3072]{1,0:T(8,128)(2,1)} %collective-permute-done.27), channel_id=1, source_target_pairs={{0,4},{4,0},{1,5},{5,1},{2,6},{6,2},{3,7},{7,3},{8,12},{12,8},{9,1... | collective-permute-start | bytes 1769480 | tf_op jit(solution)/shard_map/ppermute | solution.py:59
  199.8 54.8 %collective-permute-start.34 = (bf16[384,768]{1,0:T(8,128)(2,1)}, bf16[384,768]{1,0:T(8,128)(2,1)}, u32[]{:S(2)}, u32[]{:S(2)}) collective-permute-start(bf16[384,768]{1,0:T(8,128)(2,1)} %collective-permute-done.32), channel_id=1, source_target_pairs={{0,2},{2,0},{1,3},{3,1},{4,6},{6,4},{5,7},{7,5},{8,10},{10,8},{9,1... | collective-permute-start | bytes 1769480 | tf_op jit(solution)/shard_map/ppermute | solution.py:59
  333.4 77.0 %collective-permute-start.35 = (bf16[2,4608]{1,0:T(2,128)(2,1)S(1)}, bf16[2,4608]{1,0:T(2,128)(2,1)S(1)}, u32[]{:S(2)}, u32[]{:S(2)}) collective-permute-start(bf16[2,4608]{1,0:T(2,128)(2,1)S(1)} %constant_dynamic-update-slice_fusion.11), channel_id=1, source_target_pairs={{0,1},{1,0},{2,3},{3,2},{4,5},{5,4},{6,7},{7,6},{8,9},{9,8},{10,11... | collective-permute-start | bytes 55304 | tf_op jit(solution)/shard_map/ppermute | solution.py:59
  425.9 33.7 %collective-permute-start.54 = (bf16[8,120,128]{2,1,0:T(8,128)(2,1)S(1)}, bf16[8,120,128]{2,1,0:T(8,128)(2,1)S(1)}, u32[]{:S(2)}, u32[]{:S(2)}) collective-permute-start(bf16[8,120,128]{2,1,0:T(8,128)(2,1)S(1)} %pad_maximum_fusion.46), channel_id=1, source_target_pairs={{0,16},{8,24},{16,0},{24,8},{1,17},{9,25},{17,1},{25,9},{2,18},{10... | collective-permute-start | bytes 737288 | tf_op jit(solution)/shard_map/ppermute | solution.py:189
  427.4 34.6 %collective-permute-start.53 = (bf16[8,120,128]{2,1,0:T(8,128)(2,1)S(1)}, bf16[8,120,128]{2,1,0:T(8,128)(2,1)S(1)}, u32[]{:S(2)}, u32[]{:S(2)}) collective-permute-start(bf16[8,120,128]{2,1,0:T(8,128)(2,1)S(1)} %pad_maximum_fusion.46), channel_id=1, source_target_pairs={{0,8},{8,0},{16,24},{24,16},{1,9},{9,1},{17,25},{25,17},{2,10},{10... | collective-permute-start | bytes 737288 | tf_op jit(solution)/shard_map/ppermute | solution.py:189
  428.9 42.8 %collective-permute-start.49 = (bf16[8,120,128]{2,1,0:T(8,128)(2,1)}, bf16[8,120,128]{2,1,0:T(8,128)(2,1)}, u32[]{:S(2)}, u32[]{:S(2)}) collective-permute-start(bf16[8,120,128]{2,1,0:T(8,128)(2,1)} %pad_maximum_fusion.45), channel_id=1, source_target_pairs={{0,24},{8,16},{16,8},{24,0},{1,25},{9,17},{17,9},{25,1},{2,26},{10... | collective-permute-start | bytes 737288 | tf_op jit(solution)/shard_map/ppermute | solution.py:189
  430.2 42.4 %collective-permute-start.48 = (bf16[8,120,128]{2,1,0:T(8,128)(2,1)}, bf16[8,120,128]{2,1,0:T(8,128)(2,1)}, u32[]{:S(2)}, u32[]{:S(2)}) collective-permute-start(bf16[8,120,128]{2,1,0:T(8,128)(2,1)} %pad_maximum_fusion.45), channel_id=1, source_target_pairs={{0,16},{8,24},{16,0},{24,8},{1,17},{9,25},{17,1},{25,9},{2,18},{10... | collective-permute-start | bytes 737288 | tf_op jit(solution)/shard_map/ppermute | solution.py:189
  434.9 82.0 %collective-permute-start.89 = (bf16[768,384]{1,0:T(8,128)(2,1)}, bf16[768,384]{1,0:T(8,128)(2,1)}, u32[]{:S(2)}, u32[]{:S(2)}) collective-permute-start(bf16[768,384]{1,0:T(8,128)(2,1)} %convolution_convert_fusion.12), channel_id=1, source_target_pairs={{0,2},{2,0},{1,3},{3,1},{4,6},{6,4},{5,7},{7,5},{8,10},{10,8},{9,1... | collective-permute-start | bytes 1769480 | tf_op jit(solution)/shard_map/ppermute | solution.py:59
  459.6 178.3 %collective-permute-start.133 = (bf16[3072,384]{1,0:T(8,128)(2,1)}, bf16[3072,384]{1,0:T(8,128)(2,1)}, u32[]{:S(2)}, u32[]{:S(2)}) collective-permute-start(bf16[3072,384]{1,0:T(8,128)(2,1)} %convolution_convert_fusion), channel_id=1, source_target_pairs={{0,2},{2,0},{1,3},{3,1},{4,6},{6,4},{5,7},{7,5},{8,10},{10,8},{9,1... | collective-permute-start | bytes 7077896 | tf_op jit(solution)/shard_map/ppermute | solution.py:59
  471.6 170.8 %collective-permute-start.111 = (bf16[768,1536]{1,0:T(8,128)(2,1)}, bf16[768,1536]{1,0:T(8,128)(2,1)}, u32[]{:S(2)}, u32[]{:S(2)}) collective-permute-start(bf16[768,1536]{1,0:T(8,128)(2,1)} %convolution_convert_fusion.2), channel_id=1, source_target_pairs={{0,2},{2,0},{1,3},{3,1},{4,6},{6,4},{5,7},{7,5},{8,10},{10,8},{9,1... | collective-permute-start | bytes 7077896 | tf_op jit(solution)/shard_map/ppermute | solution.py:59
  472.6 46.3 %collective-permute-start.78 = (bf16[768,384]{1,0:T(8,128)(2,1)}, bf16[768,384]{1,0:T(8,128)(2,1)}, u32[]{:S(2)}, u32[]{:S(2)}) collective-permute-start(bf16[768,384]{1,0:T(8,128)(2,1)} %convolution_convert_fusion.13), channel_id=1, source_target_pairs={{0,2},{2,0},{1,3},{3,1},{4,6},{6,4},{5,7},{7,5},{8,10},{10,8},{9,1... | collective-permute-start | bytes 1769480 | tf_op jit(solution)/shard_map/ppermute | solution.py:59
  475.3 153.1 %collective-permute-start.67 = (bf16[768,1152]{1,0:T(8,128)(2,1)}, bf16[768,1152]{1,0:T(8,128)(2,1)}, u32[]{:S(2)}, u32[]{:S(2)}) collective-permute-start(bf16[768,1152]{1,0:T(8,128)(2,1)} %convolution_convert_fusion.4), channel_id=1, source_target_pairs={{0,2},{2,0},{1,3},{3,1},{4,6},{6,4},{5,7},{7,5},{8,10},{10,8},{9,1... | collective-permute-start | bytes 5308424 | tf_op jit(solution)/shard_map/ppermute | solution.py:59
  516.9 114.5 %collective-permute-start.56 = (bf16[768,1152]{1,0:T(8,128)(2,1)}, bf16[768,1152]{1,0:T(8,128)(2,1)S(1)}, u32[]{:S(2)}, u32[]{:S(2)}) collective-permute-start(bf16[768,1152]{1,0:T(8,128)(2,1)} %convolution_convert_fusion.5), channel_id=1, source_target_pairs={{0,2},{2,0},{1,3},{3,1},{4,6},{6,4},{5,7},{7,5},{8,10},{10,8},{9,1... | collective-permute-start | bytes 5308424 | tf_op jit(solution)/shard_map/ppermute | solution.py:59
  609.1 37.7 %collective-permute-start.100 = (bf16[768,1536]{1,0:T(8,128)(2,1)S(1)}, bf16[768,1536]{1,0:T(8,128)(2,1)S(1)}, u32[]{:S(2)}, u32[]{:S(2)}) collective-permute-start(bf16[768,1536]{1,0:T(8,128)(2,1)S(1)} %copy-done.120), channel_id=1, source_target_pairs={{0,2},{2,0},{1,3},{3,1},{4,6},{6,4},{5,7},{7,5},{8,10},{10,8},{9,1... | collective-permute-start | bytes 7077896 | tf_op jit(solution)/shard_map/ppermute | solution.py:59
  637.9 37.2 %collective-permute-start.57 = (bf16[2,4,48,1152]{3,2,1,0:T(8,128)(2,1)S(1)}, bf16[2,4,48,1152]{3,2,1,0:T(8,128)(2,1)S(1)}, u32[]{:S(2)}, u32[]{:S(2)}) collective-permute-start(bf16[2,4,48,1152]{3,2,1,0:T(8,128)(2,1)S(1)} %dynamic-slice_bitcast_fusion.4), channel_id=1, source_target_pairs={{0,1},{1,0},{2,3},{3,2},{4,5},{5,4},{6,7},{7,6},{8,9},{9,8},{10,11... | collective-permute-start | bytes 2654216 | tf_op jit(solution)/shard_map/ppermute | solution.py:59
  642.4 62.0 %collective-permute-start.134 = (bf16[2,4,192,384]{3,2,1,0:T(8,128)(2,1)S(1)}, bf16[2,4,192,384]{3,2,1,0:T(8,128)(2,1)S(1)}, u32[]{:S(2)}, u32[]{:S(2)}) collective-permute-start(bf16[2,4,192,384]{3,2,1,0:T(8,128)(2,1)S(1)} %dynamic-slice_bitcast_fusion), channel_id=1, source_target_pairs={{0,1},{1,0},{2,3},{3,2},{4,5},{5,4},{6,7},{7,6},{8,9},{9,8},{10,11... | collective-permute-start | bytes 3538952 | tf_op jit(solution)/shard_map/ppermute | solution.py:59
  646.8 59.3 %collective-permute-start.112 = (bf16[2,4,48,1536]{3,2,1,0:T(8,128)(2,1)S(1)}, bf16[2,4,48,1536]{3,2,1,0:T(8,128)(2,1)S(1)}, u32[]{:S(2)}, u32[]{:S(2)}) collective-permute-start(bf16[2,4,48,1536]{3,2,1,0:T(8,128)(2,1)S(1)} %dynamic-slice_bitcast_fusion.2), channel_id=1, source_target_pairs={{0,4},{4,0},{1,5},{5,1},{2,6},{6,2},{3,7},{7,3},{8,12},{12,8},{9,1... | collective-permute-start | bytes 3538952 | tf_op jit(solution)/shard_map/ppermute | solution.py:59
  649.8 75.9 %collective-permute-start.101 = (bf16[2,4,48,1536]{3,2,1,0:T(8,128)(2,1)S(1)}, bf16[2,4,48,1536]{3,2,1,0:T(8,128)(2,1)S(1)}, u32[]{:S(2)}, u32[]{:S(2)}) collective-permute-start(bf16[2,4,48,1536]{3,2,1,0:T(8,128)(2,1)S(1)} %dynamic-slice_bitcast_fusion.3), channel_id=1, source_target_pairs={{0,1},{1,0},{2,3},{3,2},{4,5},{5,4},{6,7},{7,6},{8,9},{9,8},{10,11... | collective-permute-start | bytes 3538952 | tf_op jit(solution)/shard_map/ppermute | solution.py:59
  656.1 71.2 %collective-permute-start.123 = (bf16[2,4,192,384]{3,2,1,0:T(8,128)(2,1)S(1)}, bf16[2,4,192,384]{3,2,1,0:T(8,128)(2,1)S(1)}, u32[]{:S(2)}, u32[]{:S(2)}) collective-permute-start(bf16[2,4,192,384]{3,2,1,0:T(8,128)(2,1)S(1)} %dynamic-slice_bitcast_fusion.1), channel_id=1, source_target_pairs={{0,4},{4,0},{1,5},{5,1},{2,6},{6,2},{3,7},{7,3},{8,12},{12,8},{9,1... | collective-permute-start | bytes 3538952 | tf_op jit(solution)/shard_map/ppermute | solution.py:59
  706.1 76.5 %collective-permute-start.135 = (bf16[3,2,192,384]{3,2,1,0:T(8,128)(2,1)S(1)}, bf16[3,2,192,384]{3,2,1,0:T(8,128)(2,1)S(1)}, u32[]{:S(2)}, u32[]{:S(2)}) collective-permute-start(bf16[3,2,192,384]{3,2,1,0:T(8,128)(2,1)S(1)} %pad_maximum_fusion.17), channel_id=1, source_target_pairs={{0,8},{24,16},{1,9},{25,17},{2,10},{26,18},{3,11},{27,19},{4,12},{... | collective-permute-start | bytes 2654216 | tf_op jit(solution)/shard_map/ppermute | solution.py:101
  725.7 28.1 %collective-permute-start.113 = (bf16[4,48,1536]{2,1,0:T(8,128)(2,1)S(1)}, bf16[4,48,1536]{2,1,0:T(8,128)(2,1)S(1)}, u32[]{:S(2)}, u32[]{:S(2)}) collective-permute-start(bf16[4,48,1536]{2,1,0:T(8,128)(2,1)S(1)} %dynamic-slice_bitcast_fusion.6), channel_id=1, source_target_pairs={{0,1},{1,0},{2,3},{3,2},{4,5},{5,4},{6,7},{7,6},{8,9},{9,8},{10,11... | collective-permute-start | bytes 1769480 | tf_op jit(solution)/shard_map/ppermute | solution.py:59
  727.3 56.2 %collective-permute-start.102 = (bf16[3,2,48,1536]{3,2,1,0:T(8,128)(2,1)S(1)}, bf16[3,2,48,1536]{3,2,1,0:T(8,128)(2,1)S(1)}, u32[]{:S(2)}, u32[]{:S(2)}) collective-permute-start(bf16[3,2,48,1536]{3,2,1,0:T(8,128)(2,1)S(1)} %pad_maximum_fusion.15), channel_id=1, source_target_pairs={{0,8},{24,16},{1,9},{25,17},{2,10},{26,18},{3,11},{27,19},{4,12},{... | collective-permute-start | bytes 2654216 | tf_op jit(solution)/shard_map/ppermute | solution.py:101
  754.3 30.1 %collective-permute-start.114 = (bf16[3,48,1536]{2,1,0:T(8,128)(2,1)S(1)}, bf16[3,48,1536]{2,1,0:T(8,128)(2,1)S(1)}, u32[]{:S(2)}, u32[]{:S(2)}) collective-permute-start(bf16[3,48,1536]{2,1,0:T(8,128)(2,1)S(1)} %pad_maximum_fusion.33), channel_id=1, source_target_pairs={{0,8},{24,16},{1,9},{25,17},{2,10},{26,18},{3,11},{27,19},{4,12},{... | collective-permute-start | bytes 1327112 | tf_op jit(solution)/shard_map/ppermute | solution.py:101
  756.4 28.9 %collective-permute-start.125 = (bf16[3,192,384]{2,1,0:T(8,128)(2,1)S(1)}, bf16[3,192,384]{2,1,0:T(8,128)(2,1)S(1)}, u32[]{:S(2)}, u32[]{:S(2)}) collective-permute-start(bf16[3,192,384]{2,1,0:T(8,128)(2,1)S(1)} %pad_maximum_fusion.35), channel_id=1, source_target_pairs={{0,8},{24,16},{1,9},{25,17},{2,10},{26,18},{3,11},{27,19},{4,12},{... | collective-permute-start | bytes 1327112 | tf_op jit(solution)/shard_map/ppermute | solution.py:101
  783.5 71.6 %collective-permute-start.136 = (bf16[2,2,192,384]{3,2,1,0:T(8,128)(2,1)S(1)}, bf16[2,2,192,384]{3,2,1,0:T(8,128)(2,1)S(1)}, u32[]{:S(2)}, u32[]{:S(2)}) collective-permute-start(bf16[2,2,192,384]{3,2,1,0:T(8,128)(2,1)S(1)} %pad_maximum_fusion.27), channel_id=1, source_target_pairs={{8,16},{16,8},{9,17},{17,9},{10,18},{18,10},{11,19},{19,11},{12,20... | collective-permute-start | bytes 1769480 | tf_op jit(solution)/shard_map/ppermute | solution.py:102
  784.4 72.0 %collective-permute-start.103 = (bf16[2,2,48,1536]{3,2,1,0:T(8,128)(2,1)S(1)}, bf16[2,2,48,1536]{3,2,1,0:T(8,128)(2,1)S(1)}, u32[]{:S(2)}, u32[]{:S(2)}) collective-permute-start(bf16[2,2,48,1536]{3,2,1,0:T(8,128)(2,1)S(1)} %pad_maximum_fusion.23), channel_id=1, source_target_pairs={{8,16},{16,8},{9,17},{17,9},{10,18},{18,10},{11,19},{19,11},{12,20... | collective-permute-start | bytes 1769480 | tf_op jit(solution)/shard_map/ppermute | solution.py:102
  786.9 49.2 %collective-permute-start.116 = (bf16[48,1536]{1,0:T(8,128)(2,1)S(1)}, bf16[48,1536]{1,0:T(8,128)(2,1)S(1)}, u32[]{:S(2)}, u32[]{:S(2)}) collective-permute-start(bf16[48,1536]{1,0:T(8,128)(2,1)S(1)} %fusion.150), channel_id=1, source_target_pairs={{8,0},{16,24},{9,1},{17,25},{10,2},{18,26},{11,3},{19,27},{12,4},{... | collective-permute-start | bytes 442376 | tf_op jit(solution)/shard_map/ppermute | solution.py:112
  788.2 98.8 %collective-permute-start.76 = (bf16[3,2,48,1152]{3,2,1,0:T(8,128)(2,1)S(1)}, bf16[3,2,48,1152]{3,2,1,0:T(8,128)(2,1)S(1)}, u32[]{:S(2)}, u32[]{:S(2)}) collective-permute-start(bf16[3,2,48,1152]{3,2,1,0:T(8,128)(2,1)S(1)} %pad_maximum_fusion.22), channel_id=1, source_target_pairs={{8,0},{16,24},{9,1},{17,25},{10,2},{18,26},{11,3},{19,27},{12,4},{... | collective-permute-start | bytes 1990664 | tf_op jit(solution)/shard_map/ppermute | solution.py:124
  789.6 63.9 %collective-permute-start.127 = (bf16[192,384]{1,0:T(8,128)(2,1)S(1)}, bf16[192,384]{1,0:T(8,128)(2,1)S(1)}, u32[]{:S(2)}, u32[]{:S(2)}) collective-permute-start(bf16[192,384]{1,0:T(8,128)(2,1)S(1)} %fusion.153), channel_id=1, source_target_pairs={{8,0},{16,24},{9,1},{17,25},{10,2},{18,26},{11,3},{19,27},{12,4},{... | collective-permute-start | bytes 442376 | tf_op jit(solution)/shard_map/ppermute | solution.py:112
  836.0 52.3 %collective-permute-start.65 = (bf16[3,2,48,1152]{3,2,1,0:T(8,128)(2,1)S(1)}, bf16[3,2,48,1152]{3,2,1,0:T(8,128)(2,1)S(1)}, u32[]{:S(2)}, u32[]{:S(2)}) collective-permute-start(bf16[3,2,48,1152]{3,2,1,0:T(8,128)(2,1)S(1)} %pad_maximum_fusion.20), channel_id=1, source_target_pairs={{8,0},{16,24},{9,1},{17,25},{10,2},{18,26},{11,3},{19,27},{12,4},{... | collective-permute-start | bytes 1990664 | tf_op jit(solution)/shard_map/ppermute | solution.py:124
  882.2 35.4 %collective-permute-start.119 = (bf16[3,48,1536]{2,1,0:T(8,128)(2,1)S(1)}, bf16[3,48,1536]{2,1,0:T(8,128)(2,1)S(1)}, u32[]{:S(2)}, u32[]{:S(2)}) collective-permute-start(bf16[3,48,1536]{2,1,0:T(8,128)(2,1)S(1)} %pad_maximum_fusion.34), channel_id=1, source_target_pairs={{8,0},{16,24},{9,1},{17,25},{10,2},{18,26},{11,3},{19,27},{12,4},{... | collective-permute-start | bytes 1327112 | tf_op jit(solution)/shard_map/ppermute | solution.py:124
  884.6 38.0 %collective-permute-start.130 = (bf16[3,192,384]{2,1,0:T(8,128)(2,1)S(1)}, bf16[3,192,384]{2,1,0:T(8,128)(2,1)S(1)}, u32[]{:S(2)}, u32[]{:S(2)}) collective-permute-start(bf16[3,192,384]{2,1,0:T(8,128)(2,1)S(1)} %pad_maximum_fusion.36), channel_id=1, source_target_pairs={{8,0},{16,24},{9,1},{17,25},{10,2},{18,26},{11,3},{19,27},{12,4},{... | collective-permute-start | bytes 1327112 | tf_op jit(solution)/shard_map/ppermute | solution.py:124
  888.3 35.2 %collective-permute-start.77 = (bf16[384,1152]{1,0:T(8,128)(2,1)S(1)}, bf16[384,1152]{1,0:T(8,128)(2,1)S(1)}, u32[]{:S(2)}, u32[]{:S(2)}) collective-permute-start(bf16[384,1152]{1,0:T(8,128)(2,1)S(1)} %bitcast.912), channel_id=1, source_target_pairs={{0,2},{2,0},{1,3},{3,1},{4,6},{6,4},{5,7},{7,5},{8,10},{10,8},{9,1... | collective-permute-start | bytes 2654216 | tf_op jit(solution)/shard_map/ppermute | solution.py:59
  933.2 39.7 %collective-permute-start.121 = (bf16[384,1536]{1,0:T(8,128)(2,1)S(1)}, bf16[384,1536]{1,0:T(8,128)(2,1)S(1)}, u32[]{:S(2)}, u32[]{:S(2)}) collective-permute-start(bf16[384,1536]{1,0:T(8,128)(2,1)S(1)} %bitcast.908), channel_id=1, source_target_pairs={{0,2},{2,0},{1,3},{3,1},{4,6},{6,4},{5,7},{7,5},{8,10},{10,8},{9,1... | collective-permute-start | bytes 3538952 | tf_op jit(solution)/shard_map/ppermute | solution.py:59
  945.9 27.2 %collective-permute-start.132 = (bf16[1536,384]{1,0:T(8,128)(2,1)S(1)}, bf16[1536,384]{1,0:T(8,128)(2,1)S(1)}, u32[]{:S(2)}, u32[]{:S(2)}) collective-permute-start(bf16[1536,384]{1,0:T(8,128)(2,1)S(1)} %bitcast.909), channel_id=1, source_target_pairs={{0,2},{2,0},{1,3},{3,1},{4,6},{6,4},{5,7},{7,5},{8,10},{10,8},{9,1... | collective-permute-start | bytes 3538952 | tf_op jit(solution)/shard_map/ppermute | solution.py:59
  (236 other events, 2048.5 us)

commit v2 on v1

v2 whole, which is shorter than its diff:
```python
import functools

import jax
import jax.numpy as jnp
import numpy as np
from jax import lax
from jax.experimental import pallas as pl
from jax.experimental.pallas import tpu as pltpu
from jax.sharding import Mesh
from jax.sharding import PartitionSpec as P

HEADS = 12
eps = 1e-06
f32 = jnp.float32
bf16 = jnp.bfloat16


def normalize(rows):
    centred = rows - jnp.mean(rows, axis=-1, keepdims=True)
    inverse = lax.rsqrt(jnp.mean(centred * centred, axis=-1, keepdims=True) + eps)
    return (centred * inverse, inverse)


def norm_back(upstream, normed, inverse):
    return inverse * (
        upstream
        - jnp.mean(upstream, axis=-1, keepdims=True)
        - normed * jnp.mean(upstream * normed, axis=-1, keepdims=True)
    )


def gelu_parts(u):
    inner = 0.7978845608028654 * (u + 0.044715 * u * u * u)
    return jnp.tanh(inner)


def gelu(u):
    return 0.5 * u * (1.0 + gelu_parts(u))


def gelu_slope(u):
    t = gelu_parts(u)
    return 0.5 * (1.0 + t) + 0.5 * u * (1.0 - t * t) * 0.7978845608028654 * (
        1.0 + 3.0 * 0.044715 * u * u
    )


def mm(a, b):
    return jnp.dot(a, b, preferred_element_type=f32)


def mm_t(a, b):
    return lax.dot_general(a, b, (((1,), (1,)), ((), ())), preferred_element_type=f32)


def t_mm(a, b):
    return lax.dot_general(a, b, (((0,), (0,)), ((), ())), preferred_element_type=f32)


def pick(array, index, axis=0):
    return lax.dynamic_index_in_dim(array, index, axis, keepdims=False)


SWAP = [(0, 1), (1, 0)]
CHEAP = pl.CostEstimate(flops=1, bytes_accessed=1, transcendentals=0)
PARAMS = pltpu.CompilerParams(vmem_limit_bytes=40 * 2**20)


def swap(value, axis):
    return lax.ppermute(value, axis, SWAP)


def gate(tree):
    values, shape = jax.tree.flatten(tree)
    count = len(values)

    def nothing(*refs):
        pass

    out = pl.pallas_call(
        nothing,
        out_shape=[jax.ShapeDtypeStruct(v.shape, v.dtype) for v in values],
        in_specs=[pl.BlockSpec(memory_space=pl.ANY)] * count,
        out_specs=[pl.BlockSpec(memory_space=pl.ANY)] * count,
        input_output_aliases={i: i for i in range(count)},
        cost_estimate=CHEAP,
    )(*values)
    return jax.tree.unflatten(shape, out)


def call(kernel, grid, ins, outs, prefetch=(), aliases=None):
    def spec(block, index, once=False):
        if block is None:
            return pl.BlockSpec(memory_space=pl.ANY)
        if once:
            return pl.BlockSpec(block, index, pipeline_mode=pl.Buffered(1))
        return pl.BlockSpec(block, index)

    return pl.pallas_call(
        kernel,
        out_shape=[jax.ShapeDtypeStruct(shape, dtype) for shape, dtype, _, _ in outs],
        grid_spec=pltpu.PrefetchScalarGridSpec(
            num_scalar_prefetch=len(prefetch),
            grid=grid,
            in_specs=[spec(*entry[1:]) for entry in ins],
            out_specs=[spec(block, index) for _, _, block, index in outs],
        ),
        input_output_aliases=aliases or {},
        cost_estimate=CHEAP,
        compiler_params=PARAMS,
    )(*prefetch, *[entry[0] for entry in ins])


class Block:
    def __init__(self, mod, biases, seq_count, length):
        self.mod = mod.reshape(seq_count, 6, -1)
        self.biases = biases
        self.seq_count, self.length = seq_count, length
        self.features = self.mod.shape[2]

    def rows(self, array):
        return (array, (self.length, array.shape[1]), lambda s: (s, 0))

    def rows_out(self, width, dtype):
        shape = (self.seq_count * self.length, width)
        return (shape, dtype, (self.length, width), lambda s: (s, 0))

    def mods(self):
        return (self.mod, (None, 6, self.features), lambda s: (s, 0, 0))

    def sums_out(self):
        return (
            (self.seq_count, 8, self.features),
            f32,
            (None, 8, self.features),
            lambda s: (s, 0, 0),
        )

    @staticmethod
    def whole(array):
        return (array, array.shape, lambda s: (0,) * array.ndim, True)

    def attention(self, stream, w_qkv):
        bias_qv, features = self.biases[0], self.features
        bias = jnp.concatenate(
            [bias_qv[:features], jnp.zeros((features,), f32), bias_qv[features:]]
        )[None]

        def kernel(stream_ref, mod_ref, w_ref, bias_ref, in_ref, qkv_ref):
            normed, _ = normalize(stream_ref[...])
            attn_in = (normed * (1.0 + mod_ref[1:2]) + mod_ref[0:1]).astype(bf16)
            in_ref[...] = attn_in
            qkv_ref[...] = (mm(attn_in, w_ref[...]) + bias_ref[...]).astype(bf16)

        self.stream = stream
        self.attn_in, self.qkv = call(
            kernel,
            (self.seq_count,),
            [self.rows(stream), self.mods(), self.whole(w_qkv), self.whole(bias)],
            [self.rows_out(features, bf16), self.rows_out(3 * features, bf16)],
        )
        self.attn_out = attention_forward(self.qkv, self.seq_count)

    def project(self, w_out):
        def kernel(out_ref, stream_ref, mod_ref, w_ref, bias_ref, branch_ref, middle_ref, in_ref):
            branch = mm(out_ref[...], w_ref[...]) + bias_ref[...]
            middle = stream_ref[...] + mod_ref[2:3] * branch
            normed, _ = normalize(middle)
            branch_ref[...] = branch
            middle_ref[...] = middle
            in_ref[...] = (normed * (1.0 + mod_ref[4:5]) + mod_ref[3:4]).astype(bf16)

        self.branch, self.middle, self.mlp_in = call(
            kernel,
            (self.seq_count,),
            [
                self.rows(self.attn_out),
                self.rows(self.stream),
                self.mods(),
                self.whole(w_out),
                self.whole(self.biases[1][None]),
            ],
            [
                self.rows_out(self.features, f32),
                self.rows_out(self.features, f32),
                self.rows_out(self.features, bf16),
            ],
        )

    def wide(self, array, tile):
        return (array, (self.length, tile), lambda j, s: (s, j))

    def hidden_layer(self, w_fc1):
        hidden, tile = w_fc1.shape[1], self.features
        shape = (self.seq_count * self.length, hidden)

        def kernel(in_ref, w_ref, bias_ref, pre_ref, hidden_ref):
            pre = mm(in_ref[...], w_ref[...]) + bias_ref[...]
            pre_ref[...] = pre
            hidden_ref[...] = gelu(pre).astype(bf16)

        self.hidden_pre, self.hidden = call(
            kernel,
            (hidden // tile, self.seq_count),
            [
                (self.mlp_in, (self.length, self.features), lambda j, s: (s, 0)),
                (w_fc1, (self.features, tile), lambda j, s: (0, j)),
                (self.biases[2][None], (1, tile), lambda j, s: (0, j)),
            ],
            [
                (shape, f32, (self.length, tile), lambda j, s: (s, j)),
                (shape, bf16, (self.length, tile), lambda j, s: (s, j)),
            ],
        )

    def output_layer(self, w_fc2, dtype):
        def kernel(hidden_ref, middle_ref, mod_ref, w_ref, bias_ref, output_ref, stream_ref):
            output = mm(hidden_ref[...], w_ref[...]) + bias_ref[...]
            output_ref[...] = output
            stream_ref[...] = (middle_ref[...] + mod_ref[5:6] * output).astype(dtype)

        self.output, stream = call(
            kernel,
            (self.seq_count,),
            [
                self.rows(self.hidden),
                self.rows(self.middle),
                self.mods(),
                self.whole(w_fc2),
                self.whole(self.biases[3][None]),
            ],
            [self.rows_out(self.features, f32), self.rows_out(self.features, dtype)],
        )
        return stream

    def back_start(self, dh):
        def kernel(dh_ref, mod_ref, grad_ref, sums_ref):
            grad_out = (mod_ref[5:6] * dh_ref[...].astype(f32)).astype(bf16)
            grad_ref[...] = grad_out
            sums_ref[0:1] = jnp.sum(grad_out.astype(f32), axis=0, keepdims=True)

        self.dh = dh
        self.grad_out, self.sums_out2 = call(
            kernel,
            (self.seq_count,),
            [self.rows(dh), self.mods()],
            [self.rows_out(self.features, bf16), self.sums_out()],
        )
        return (self.hidden, self.grad_out)

    def back_hidden(self, w_fc2):
        hidden, tile = w_fc2.shape[0], self.features
        shape = (self.seq_count * self.length, hidden)

        def kernel(grad_ref, pre_ref, w_ref, out_ref, sum_ref):
            grad_hidden = mm_t(grad_ref[...], w_ref[...])
            grad_pre = (grad_hidden * gelu_slope(pre_ref[...])).astype(bf16)
            out_ref[...] = grad_pre
            sum_ref[...] = jnp.sum(grad_pre.astype(f32), axis=0, keepdims=True)

        self.grad_pre, self.sum_fc1 = call(
            kernel,
            (hidden // tile, self.seq_count),
            [
                (self.grad_out, (self.length, self.features), lambda j, s: (s, 0)),
                self.wide(self.hidden_pre, tile),
                (w_fc2, (tile, self.features), lambda j, s: (j, 0)),
            ],
            [
                (shape, bf16, (self.length, tile), lambda j, s: (s, j)),
                ((self.seq_count, 1, hidden), f32, (None, 1, tile), lambda j, s: (s, 0, j)),
            ],
        )
        return (self.mlp_in, self.grad_pre)

    def back_middle(self, w_fc1, w_out):
        def kernel(
            grad_ref, w1_ref, dh_ref, output_ref, middle_ref, mod_ref, branch_ref, wo_ref,
            mid_ref, gb_ref, ga_ref, sums_ref,
        ):
            grad_in = mm_t(grad_ref[...], w1_ref[...])
            normed, inverse = normalize(middle_ref[...])
            dh = dh_ref[...].astype(f32)
            mid = dh + norm_back(grad_in * (1.0 + mod_ref[4:5]), normed, inverse)
            grad_branch = (mod_ref[2:3] * mid).astype(bf16)
            mid_ref[...] = mid
            gb_ref[...] = grad_branch
            ga_ref[...] = mm_t(grad_branch, wo_ref[...]).astype(bf16)
            for at, value in enumerate(
                (
                    mid * branch_ref[...],
                    grad_in,
                    grad_in * normed,
                    dh * output_ref[...],
                    grad_branch.astype(f32),
                )
            ):
                sums_ref[at : at + 1] = jnp.sum(value, axis=0, keepdims=True)

        self.grad_mid, self.grad_branch, self.grad_attn, self.sums_mid = call(
            kernel,
            (self.seq_count,),
            [
                self.rows(self.grad_pre),
                self.whole(w_fc1),
                self.rows(self.dh),
                self.rows(self.output),
                self.rows(self.middle),
                self.mods(),
                self.rows(self.branch),
                self.whole(w_out),
            ],
            [
                self.rows_out(self.features, f32),
                self.rows_out(self.features, bf16),
                self.rows_out(self.features, bf16),
                self.sums_out(),
            ],
        )
        return (self.attn_out, self.grad_branch)

    def back_attention(self):
        self.grad_qkv = attention_backward(self.qkv, self.grad_attn, self.seq_count)
        return (self.attn_in, self.grad_qkv)

    def back_end(self, w_qkv):
        features = self.features

        def kernel(grad_ref, w_ref, stream_ref, mod_ref, mid_ref, dh_ref, sums_ref):
            grad_qkv = grad_ref[...]
            grad_in = mm_t(grad_qkv, w_ref[...])
            normed, inverse = normalize(stream_ref[...].astype(f32))
            dh_ref[...] = mid_ref[...] + norm_back(
                grad_in * (1.0 + mod_ref[1:2]), normed, inverse
            )
            for at, value in enumerate((grad_in, grad_in * normed)):
                sums_ref[at : at + 1] = jnp.sum(value, axis=0, keepdims=True)
            for part in range(3):
                columns = grad_qkv[:, part * features : (part + 1) * features].astype(f32)
                sums_ref[2 + part : 3 + part] = jnp.sum(columns, axis=0, keepdims=True)

        dh, sums = call(
            kernel,
            (self.seq_count,),
            [
                self.rows(self.grad_qkv),
                self.whole(w_qkv),
                self.rows(self.stream),
                self.mods(),
                self.rows(self.grad_mid),
            ],
            [self.rows_out(features, f32), self.sums_out()],
        )
        grad_mod = jnp.concatenate([sums[:, 0:2], self.sums_mid[:, 0:4]], axis=1)
        grad_mod = grad_mod.reshape(self.seq_count, 6 * features).astype(bf16)
        totals = jnp.sum(sums, axis=0)
        bias_sums = jnp.concatenate(
            [
                totals[2],
                totals[4],
                jnp.sum(self.sums_mid[:, 4], axis=0),
                jnp.sum(self.sum_fc1[:, 0], axis=0),
                jnp.sum(self.sums_out2[:, 0], axis=0),
            ]
        ).astype(bf16)
        return dh, grad_mod, bias_sums


def softmax_of(q, k, factor):
    scores = mm_t(q, k) * factor
    raised = jnp.exp(scores - jnp.max(scores, axis=-1, keepdims=True))
    return raised * (1.0 / jnp.sum(raised, axis=-1, keepdims=True))


def head_masks(rows, head):
    lane = lax.broadcasted_iota(jnp.int32, (rows, 128), 1)
    return [jnp.logical_and(lane >= at, lane < at + head) for at in range(0, 128, head)]


def attention_forward(qkv, count):
    tokens, triple = qkv.shape
    width, length = triple // 3, tokens // count
    groups, head = width // 128, width // HEADS
    factor = head ** (-0.5)

    def kernel(q_ref, k_ref, v_ref, out_ref):
        q, k, v = q_ref[...], k_ref[...], v_ref[...]
        total = jnp.zeros((length, 128), f32)
        for mask in head_masks(length, head):
            probs = softmax_of(jnp.where(mask, q, 0), k, factor).astype(bf16)
            total = total + mm(probs, jnp.where(mask, v, 0))
        out_ref[...] = total.astype(bf16)

    def part(which):
        return pl.BlockSpec((length, 128), lambda s, g: (s, which * groups + g))

    return pl.pallas_call(
        kernel,
        out_shape=jax.ShapeDtypeStruct((tokens, width), bf16),
        grid=(count, groups),
        in_specs=[part(0), part(1), part(2)],
        out_specs=part(0),
        cost_estimate=CHEAP,
    )(qkv, qkv, qkv)


def attention_backward(qkv, grad, count):
    tokens, triple = qkv.shape
    width, length = triple // 3, tokens // count
    groups, head = width // 128, width // HEADS
    factor = head ** (-0.5)

    def kernel(q_ref, k_ref, v_ref, g_ref, out_ref):
        q, k, v, g = q_ref[...], k_ref[...], v_ref[...], g_ref[...]
        grad_q = jnp.zeros((length, 128), f32)
        grad_k = jnp.zeros((length, 128), f32)
        grad_v = jnp.zeros((length, 128), f32)
        for mask in head_masks(length, head):
            own_q, own_g = jnp.where(mask, q, 0), jnp.where(mask, g, 0)
            probs = softmax_of(own_q, k, factor)
            grad_probs = mm_t(own_g, v)
            row_terms = jnp.sum(grad_probs * probs, axis=-1, keepdims=True)
            grad_scores = (probs * (grad_probs - row_terms)).astype(bf16)
            grad_q = grad_q + mm(grad_scores, jnp.where(mask, k, 0))
            grad_k = grad_k + t_mm(grad_scores, own_q)
            grad_v = grad_v + t_mm(probs.astype(bf16), own_g)
        at = pl.program_id(1) * 128
        for part, value in enumerate((grad_q * factor, grad_k * factor, grad_v)):
            columns = pl.ds(pl.multiple_of(part * width + at, 128), 128)
            out_ref[:, columns] = value.astype(bf16)

    def part(which):
        return pl.BlockSpec((length, 128), lambda s, g: (s, which * groups + g))

    return pl.pallas_call(
        kernel,
        out_shape=jax.ShapeDtypeStruct((tokens, triple), bf16),
        grid=(count, groups),
        in_specs=[part(0), part(1), part(2), part(0)],
        out_specs=pl.BlockSpec((length, triple), lambda s, g: (s, 0)),
        cost_estimate=CHEAP,
    )(qkv, qkv, qkv, grad)


TILE = 384


def product_part(lhs, rhs, row_part, col_half, got=None, into=None, at=0, width=None):
    tokens, rows = lhs.shape
    half = rhs.shape[1] // 2
    row_at, row_count = row_part
    rows = rows // row_count
    width = width or half
    place = jnp.stack([jnp.asarray(row_at, jnp.int32), jnp.asarray(col_half, jnp.int32)])
    row_tiles, col_tiles, shift = rows // TILE, half // TILE, at // TILE
    ins = [
        (lhs, (tokens, TILE), lambda j, i, p: (0, p[0] * row_tiles + i)),
        (rhs, (tokens, TILE), lambda j, i, p: (0, p[1] * col_tiles + j)),
    ]
    if got is not None:
        ins.append((got, (TILE, TILE), lambda j, i, p: (p[0] * row_tiles + i, shift + j)))
    aliases = {}
    if into is not None:
        aliases = {1 + len(ins): 0}
        ins.append((into, None, None))

    def kernel(place_ref, lhs_ref, rhs_ref, *refs):
        total = t_mm(lhs_ref[...], rhs_ref[...])
        if got is not None:
            total = total + refs[0][...].astype(f32)
        refs[-1][...] = total.astype(bf16)

    return call(
        kernel,
        (col_tiles, row_tiles),
        ins,
        [((rows, width), bf16, (TILE, TILE), lambda j, i, p: (i, shift + j))],
        prefetch=(place,),
        aliases=aliases,
    )[0]


def unit_part(pairs, row_part, col_half, got=None):
    width = sum(rhs.shape[1] // 2 for _, rhs in pairs)
    out, at = None, 0
    for lhs, rhs in pairs:
        out = product_part(lhs, rhs, row_part, col_half, got, out, at, width)
        at += rhs.shape[1] // 2
    return out


class Fast:
    def __init__(self):
        self.near = lax.axis_index("near")
        self.core = lax.axis_index("core")
        self.shard = lax.axis_index("shard")
        self.place = jnp.stack([self.shard, self.near, self.core]).astype(jnp.int32)

    def ordered(self, mine, got, axis, at=0):
        first = lax.axis_index(axis) == 0
        return jnp.stack([jnp.where(first, mine, got), jnp.where(first, got, mine)], axis=at)

    def split(self, stack, axis, at=0):
        me = lax.axis_index(axis)
        return pick(stack, 1 - me, at), pick(stack, me, at)

    def quarter(self, stacked, layer):
        size = stacked.shape[1] // 4
        start = (self.near * 2 + self.core) * size
        return lax.dynamic_slice(stacked, (layer, start, 0), (1, size, stacked.shape[2]))[0]

    def assemble(self, stacked, layer, pieces, column):
        _, rows, width = stacked.shape
        size = rows // 4
        across = column // width

        def out_block(step, place):
            shard, near, core = place[0], place[1], place[2]
            piece = jnp.maximum(step - 4, 0)
            near_at = jnp.where(piece % 2 == 0, near, 1 - near)
            core_at = jnp.where(piece < 2, core, 1 - core)
            theirs = (1 - shard) * 4 + near_at * 2 + core_at
            return jnp.where(step < 4, shard * 4 + step, theirs), 0

        def kernel(place_ref, own_ref, *refs):
            step, out_ref = pl.program_id(0), refs[-1]

            @pl.when(step < 4)
            def _():
                out_ref[...] = own_ref[...]

            for at in range(4):

                @pl.when(step == 4 + at)
                def _(value=refs[at]):
                    out_ref[...] = value[...]

        ins = [
            (
                stacked,
                (None, size, width),
                lambda s, p: (layer, jnp.minimum(s, 3), 0),
            )
        ]
        ins += [(piece, (size, width), lambda s, p: (0, across)) for piece in pieces]
        return call(
            kernel,
            (8,),
            ins,
            [((2 * rows, width), stacked.dtype, (size, width), out_block)],
            prefetch=(self.place,),
        )[0]

    def final(self, pieces, layer, column, width, into):
        rows = pieces[0].shape[0]
        tiles, shift = width // TILE, column // TILE

        def out_block(j, piece, place):
            near, core = place[1], place[2]
            near_at = jnp.where(piece % 2 == 0, near, 1 - near)
            core_at = jnp.where(piece < 2, core, 1 - core)
            return layer, near_at, core_at * tiles + j

        def kernel(place_ref, *refs):
            piece, out_ref = pl.program_id(1), refs[-1]
            for at in range(4):

                @pl.when(piece == at)
                def _(value=refs[at]):
                    out_ref[...] = value[...].astype(f32)

        ins = [(piece, (rows, TILE), lambda j, i, p: (0, shift + j)) for piece in pieces]
        aliases = {}
        if into is not None:
            aliases = {5: 0}
            ins.append((into, None, None))
        return call(
            kernel,
            (tiles, 4),
            ins,
            [((2, 2 * rows, 2 * width), f32, (None, rows, TILE), out_block)],
            prefetch=(self.place,),
            aliases=aliases,
        )[0]


def ada_weight(silu, mods, layer, layers, into):
    count, rows = silu.shape
    width = mods.shape[1]
    tile = 768 if width % 768 == 0 else width

    def kernel(silu_ref, mods_ref, *refs):
        refs[-1][...] = t_mm(silu_ref[...], mods_ref[...])

    ins = [
        (silu, (count, rows), lambda j: (0, 0)),
        (mods, (count, tile), lambda j: (0, j)),
    ]
    aliases = {}
    if into is not None:
        aliases = {2: 0}
        ins.append((into, None, None))
    return call(
        kernel,
        (width // tile,),
        ins,
        [((layers, rows, width), f32, (None, rows, tile), lambda j: (layer, 0, j))],
        aliases=aliases,
    )[0]


def silu_grad(cond_value, grad_silu):
    _, silu_pull = jax.vjp(jax.nn.silu, cond_value)
    return silu_pull(grad_silu)[0]


def owned_biases(mod_every, bias_sums, shard, widths, shard_count):
    totals, at = [jnp.sum(mod_every.astype(f32), axis=0)], 0
    for width in widths[1:]:
        totals.append(bias_sums[at : at + width * shard_count])
        at += width * shard_count
    return [
        lax.dynamic_slice_in_dim(total, shard * width, width, 0)
        for total, width in zip(totals, widths)
    ]


def unpack_biases(bias_all, widths):
    cuts = np.cumsum(widths)[:-1]
    parts = [
        jnp.moveaxis(part, 0, 1).reshape(bias_all.shape[1], -1).astype(f32)
        for part in jnp.split(bias_all, cuts, axis=2)
    ]
    return [[part[l] for part in parts] for l in range(bias_all.shape[1])]


def in_order(outputs, dh, condition_grad, g_w_ada, biases, weights):
    return (
        outputs,
        dh,
        condition_grad,
        g_w_ada,
        biases[0],
        weights[0],
        biases[1],
        weights[1],
        biases[2],
        weights[2],
        biases[3],
        weights[3],
        biases[4],
    )


def local_plain(
    latents,
    condition,
    output_grad,
    w_ada,
    b_ada,
    query_key_value_weight,
    b_qv,
    output_matrix_weight,
    b_proj,
    first_linear_weight,
    b_fc1,
    second_linear_weight,
    b_fc2,
):
    layer_count, owned_rows, ada_width = w_ada.shape
    seq_count, length, features = latents.shape
    shard, shards = lax.axis_index("shard"), lax.axis_size("shard")
    every = ("far", "near", "core", "shard")
    biases = (b_ada, b_qv, b_proj, b_fc1, b_fc2)
    widths = [b.shape[1] for b in biases]

    cond_value = condition.astype(f32)
    silu_low = jax.nn.silu(cond_value).astype(bf16)
    silu_group = lax.all_gather(silu_low, "shard", axis=0, tiled=True)
    silu_mine = lax.dynamic_slice_in_dim(silu_group, shard * owned_rows, owned_rows, 1)
    bias_all = lax.all_gather(jnp.concatenate(biases, axis=1), "shard", axis=0)
    full_biases = unpack_biases(bias_all, widths)
    mod_part = jnp.concatenate([mm(silu_mine, w_ada[l]) for l in range(layer_count)], axis=1)
    mod = lax.psum_scatter(mod_part, "shard", scatter_dimension=0, tiled=True)
    mod = mod.reshape(seq_count, layer_count, ada_width)
    silu_every = lax.all_gather(silu_low, every, axis=0, tiled=True)

    tokens = seq_count * length
    stream, blocks, weights = latents.astype(f32).reshape(tokens, features), [], []
    for l in range(layer_count):
        block = Block(mod[:, l] + full_biases[l][0], full_biases[l][1:], seq_count, length)
        full = [
            lax.all_gather(w[l], "shard", axis=0, tiled=True)
            for w in (
                query_key_value_weight,
                output_matrix_weight,
                first_linear_weight,
                second_linear_weight,
            )
        ]
        block.attention(stream, full[0])
        block.project(full[1])
        block.hidden_layer(full[2])
        stream = block.output_layer(full[3], bf16 if l == layer_count - 1 else f32)
        blocks.append(block)
        weights.append(full)

    def reduce(pair):
        grad = t_mm(*pair).astype(bf16)
        grad = lax.psum_scatter(grad, "shard", scatter_dimension=0, tiled=True)
        return lax.psum(grad, ("far", "near", "core")).astype(f32)

    dh = output_grad.reshape(tokens, features)
    grads, ada, owned, grad_silu = [None] * layer_count, None, [None] * layer_count, 0.0
    silu_owned = lax.dynamic_slice_in_dim(silu_every, shard * owned_rows, owned_rows, 1)
    for l in reversed(range(layer_count)):
        block, full = blocks[l], weights[l]
        second = block.back_start(dh)
        first = block.back_hidden(full[3])
        out = block.back_middle(full[2], full[1])
        qkv = block.back_attention()
        dh, grad_mod, bias_sums = block.back_end(full[0])
        grads[l] = [reduce(pair) for pair in (qkv, out, first, second)]
        mod_every = lax.all_gather(grad_mod, every, axis=0, tiled=True)
        ada = ada_weight(silu_owned, mod_every, l, layer_count, ada)
        sums = lax.psum(bias_sums.astype(f32), every)
        owned[l] = owned_biases(mod_every, sums, shard, widths, shards)
        mods_group = lax.all_gather(grad_mod, "shard", axis=0, tiled=True)
        grad_silu = grad_silu + mm_t(mods_group, w_ada[l])
    by_owner = grad_silu.reshape(shards, seq_count, owned_rows)
    got = lax.all_to_all(by_owner, "shard", 0, 0)
    grad_silu = jnp.moveaxis(got, 0, 1).reshape(seq_count, features)
    return in_order(
        stream.reshape(latents.shape),
        dh.reshape(latents.shape),
        silu_grad(cond_value, grad_silu),
        ada,
        [jnp.stack([o[m] for o in owned]) for m in range(5)],
        [jnp.stack([g[m] for g in grads]) for m in range(4)],
    )


def local_fast(
    latents,
    condition,
    output_grad,
    w_ada,
    b_ada,
    query_key_value_weight,
    b_qv,
    output_matrix_weight,
    b_proj,
    first_linear_weight,
    b_fc1,
    second_linear_weight,
    b_fc2,
):
    comm = Fast()
    layer_count, owned_rows, ada_width = w_ada.shape
    seq_count, length, features = latents.shape
    tokens = seq_count * length
    shard = comm.shard
    biases = (b_ada, b_qv, b_proj, b_fc1, b_fc2)
    widths = [b.shape[1] for b in biases]

    chunk_of = []
    for l in range(layer_count):
        chunk_of.append((l, (query_key_value_weight, output_matrix_weight)))
        chunk_of.append((l, (first_linear_weight,)))
        chunk_of.append((l, (second_linear_weight,)))
    chunks = len(chunk_of)
    sends = []
    for l, members in chunk_of:
        quarters = [comm.quarter(member, l) for member in members]
        sends.append(quarters[0] if len(quarters) == 1 else jnp.concatenate(quarters, axis=1))

    cond_value = condition.astype(f32)
    silu_low = jax.nn.silu(cond_value).astype(bf16)
    bias_mine = jnp.concatenate(biases, axis=1)
    latents_flat = latents.reshape(tokens, features)
    stream = latents_flat
    pieces = [[None] * 4 for _ in range(chunks)]
    weights = [None] * chunks
    blocks = [None] * layer_count
    silu_all = silu_low.reshape(1, -1, 128)
    outputs = None
    for step in range(0, chunks + 2):
        live = {}
        if step < chunks:
            live["a"] = swap(sends[step], "shard")
        at = step - 1
        if 0 <= at < chunks:
            live["b"] = swap(pieces[at][0], "near")
            live["a2"] = swap(pieces[at][0], "core")
        at = step - 2
        if 0 <= at < chunks:
            live["b2"] = swap(pieces[at][1], "core")
        if step == 0:
            live["silu"] = swap(silu_low, "shard")
            live["bias"] = swap(bias_mine, "shard")
        elif step == 1:
            live["mod"] = swap(mod_send, "shard")
        elif step in (2, 3, 4):
            live["every"] = swap(silu_all, ("core", "shard", "near")[step - 2])
        elif step == 5:
            live["every"] = [
                lax.ppermute(silu_all, "far", [(i, i ^ k) for i in range(4)]) for k in (1, 2, 3)
            ]
        at = step - 3
        if at >= 0:
            l, part = at // 3, at % 3
            block = blocks[l]
            if part == 0:
                block.attention(stream, weights[at][0])
                block.project(weights[at][1])
                live["done"] = block.mlp_in
            elif part == 1:
                block.hidden_layer(weights[at][0])
                live["done"] = block.hidden
            else:
                stream = block.output_layer(weights[at][0], f32)
                live["done"] = stream
        if step + 1 < chunks:
            live["send"] = sends[step + 1]
        live = gate(live)
        if step + 1 < chunks:
            sends[step + 1] = live["send"]
        if step < chunks:
            pieces[step][0] = live["a"]
        if at >= 0:
            if part == 0:
                block.mlp_in = live["done"]
            elif part == 1:
                block.hidden = live["done"]
            else:
                stream = live["done"]
        at = step - 1
        if 0 <= at < chunks:
            pieces[at][1], pieces[at][2] = live["b"], live["a2"]
        at = step - 2
        if 0 <= at < chunks:
            pieces[at][3] = live["b2"]
            column, weights[at] = 0, []
            l, members = chunk_of[at]
            for member in members:
                weights[at].append(comm.assemble(member, l, pieces[at], column))
                column += member.shape[2]
        if step == 0:
            full_biases = unpack_biases(comm.ordered(bias_mine, live["bias"], "shard"), widths)
            silu_pair = comm.ordered(silu_low, live["silu"], "shard")
            silu_pair = silu_pair.reshape(2 * seq_count, features)
            silu_mine = lax.dynamic_slice_in_dim(silu_pair, shard * owned_rows, owned_rows, 1)
            mod_part = jnp.concatenate(
                [mm(silu_mine, w_ada[l]) for l in range(layer_count)], axis=1
            )
            mod_send, mod_keep = comm.split(mod_part.reshape(2, seq_count, -1), "shard")
        elif step == 1:
            mod = (mod_keep + live["mod"]).reshape(seq_count, layer_count, ada_width)
            for l in range(layer_count):
                blocks[l] = Block(
                    mod[:, l] + full_biases[l][0], full_biases[l][1:], seq_count, length
                )
            stream = stream.astype(f32)
        elif step in (2, 3, 4):
            silu_all = jnp.concatenate([silu_all, live["every"]], 0)
        elif step == 5:
            silu_all = jnp.concatenate([silu_all] + live["every"], 0)
    silu_every = silu_all.reshape(-1, features)
    silu_owned = lax.dynamic_slice_in_dim(silu_every, shard * owned_rows, owned_rows, 1)

    units = 3 * layer_count
    first_send, keep, total, late = [[None] * units for _ in range(4)]
    done = [[None] * 4 for _ in range(units)]
    grad_mods, small = [None] * layer_count, [None] * layer_count
    mod_every, bias_sums = [None] * layer_count, [None] * layer_count
    small_from = [units - 3 * l for l in range(layer_count)]
    dh = output_grad.reshape(tokens, features)
    weight_out, ada = [None] * 4, None
    chain = None
    last_mods, last_silu = units, units + 1
    for step in range(0, units + 6):
        live = {}
        at = step - 1
        if 0 <= at < units:
            live["shard"] = swap(first_send[at], "shard")
        at = step - 2
        if 0 <= at < units:
            live["near"] = swap(late[at], "near")
        at = step - 3
        if 0 <= at < units:
            if chain is not None:
                total[at], total[at - 1] = gate((total[at], chain))
            chain = total[at] = lax.psum(total[at], "far")
        at = step - 4
        if 0 <= at < units:
            live["far"] = total[at]
        at = step - 5
        if 0 <= at < units:
            live["near_back"] = swap(done[at][0], "near")
            live["core_back"] = swap(done[at][0], "core")
        at = step - 6
        if 0 <= at < units:
            live["both_back"] = swap(done[at][1], "core")
        for l in range(layer_count):
            stage = step - small_from[l]
            if 0 <= stage < 3:
                live["small", l] = swap(small[l], ("core", "shard", "near")[stage])
            elif stage == 3:
                live["small", l] = [
                    lax.ppermute(small[l], "far", [(i, i ^ k) for i in range(4)])
                    for k in (1, 2, 3)
                ]
        if step == last_mods:
            live["mods"] = swap(jnp.stack(grad_mods), "shard")
        elif step == last_silu:
            live["silu"] = swap(silu_send, "shard")
        if step < units:
            l, part = layer_count - 1 - step // 3, step % 3
            block = blocks[l]
            w_qkv, w_out = weights[3 * l]
            w_fc1, w_fc2 = weights[3 * l + 1][0], weights[3 * l + 2][0]
            if part == 0:
                pairs = [block.back_start(dh)]
                live["next"] = block.grad_out
            elif part == 1:
                pairs = [block.back_hidden(w_fc2)]
                live["next"] = block.grad_pre
            else:
                pairs = [block.back_middle(w_fc1, w_out), block.back_attention()]
            got = swap(unit_part(pairs, (0, 1), 1 - comm.core), "core")
            if part == 0 and l == layer_count - 1:
                outputs = block.output_layer(w_fc2, bf16)
            live["send"] = unit_part(pairs, (1 - shard, 2), comm.core, got)
            keep[step] = unit_part(pairs, (shard, 2), comm.core, got)
            live["keep"] = keep[step]
            if part == 2:
                dh, grad_mods[l], sums = block.back_end(w_qkv)
                small[l] = jnp.concatenate(
                    [grad_mods[l].reshape(-1, 128), sums.reshape(-1, 128)], 0
                )
                live["next"] = (dh, small[l])
        live = gate({str(key): value for key, value in live.items()})
        if step < units:
            first_send[step], keep[step] = live["send"], live["keep"]
            if part == 0:
                block.grad_out = live["next"]
            elif part == 1:
                block.grad_pre = live["next"]
            else:
                dh, small[l] = live["next"]
        at = step - 1
        if 0 <= at < units:
            shape = (2, keep[at].shape[0] // 2, keep[at].shape[1])
            sent, kept = comm.split(keep[at].reshape(shape), "near")
            got_sent, got_kept = comm.split(live["shard"].reshape(shape), "near")
            late[at] = (sent.astype(f32) + got_sent.astype(f32)).astype(bf16)
            total[at] = (kept.astype(f32) + got_kept.astype(f32)).astype(bf16)
        at = step - 2
        if 0 <= at < units:
            total[at] = (total[at].astype(f32) + live["near"].astype(f32)).astype(bf16)
        at = step - 4
        if 0 <= at < units:
            done[at][0] = live["far"]
            if chain is total[at]:
                chain = live["far"]
        at = step - 5
        if 0 <= at < units:
            done[at][1], done[at][2] = live["near_back"], live["core_back"]
        at = step - 6
        if 0 <= at < units:
            done[at][3] = live["both_back"]
        for at in [step - 6] if step - 6 < units - 1 else []:
            if at >= 0:
                weight_out = finish(comm, done[at], at, layer_count, features, weight_out)
        mod_rows = seq_count * ada_width // 128
        bias_rows = 2 * sum(widths[1:]) // 128
        for l in range(layer_count):
            stage = step - small_from[l]
            if stage == 0:
                mod_every[l], bias_sums[l] = small[l][:mod_rows], small[l][mod_rows:]
            if 0 <= stage < 3:
                got = live[str(("small", l))]
                mod_every[l] = jnp.concatenate([mod_every[l], got[:-bias_rows]], 0)
                bias_sums[l] = (
                    bias_sums[l].astype(f32) + got[-bias_rows:].astype(f32)
                ).astype(bf16)
                small[l] = jnp.concatenate([mod_every[l], bias_sums[l]], 0)
            elif stage == 3:
                got = live[str(("small", l))]
                mod_every[l] = jnp.concatenate([mod_every[l]] + [g[:-bias_rows] for g in got], 0)
                mod_every[l] = mod_every[l].reshape(-1, ada_width)
                total_sums = bias_sums[l].astype(f32)
                for g in got:
                    total_sums = total_sums + g[-bias_rows:].astype(f32)
                bias_sums[l] = total_sums.reshape(-1)
                ada = ada_weight(silu_owned, mod_every[l], l, layer_count, ada)
        if step == last_mods:
            mods_both = comm.ordered(jnp.stack(grad_mods), live["mods"], "shard")
            silu_part = functools.reduce(
                jnp.add,
                [
                    mm_t(mods_both[:, l].reshape(2 * seq_count, ada_width), w_ada[l])
                    for l in range(layer_count)
                ],
            )
            silu_send, silu_keep = comm.split(
                silu_part.reshape(2, seq_count, owned_rows), "shard"
            )
        elif step == last_silu:
            grad_silu = comm.ordered(silu_keep, live["silu"], "shard", at=1)
            grad_silu = grad_silu.reshape(seq_count, features)
    at = units - 1
    done[at][3] = swap(done[at][1], "core")
    weight_out = finish(comm, done[at], at, layer_count, features, weight_out)
    owned = [
        owned_biases(mod_every[l], bias_sums[l], shard, widths, 2) for l in range(layer_count)
    ]
    return in_order(
        outputs.reshape(latents.shape),
        dh.reshape(latents.shape),
        silu_grad(cond_value, grad_silu),
        ada,
        [jnp.stack([o[m] for o in owned]) for m in range(5)],
        weight_out,
    )


def finish(comm, pieces, unit, layer_count, features, weight_out):
    layer, part = layer_count - 1 - unit // 3, unit % 3
    width = pieces[0].shape[1]
    qkv, out, first, second = weight_out
    if part == 0:
        second = comm.final(pieces, layer, 0, width, second)
    elif part == 1:
        first = comm.final(pieces, layer, 0, width, first)
    else:
        out = comm.final(pieces, layer, 0, features // 2, out)
        qkv = comm.final(pieces, layer, features // 2, width - features // 2, qkv)
    return [qkv, out, first, second]


def solution(mesh):
    rep, shard = mesh.shape["rep"], mesh.shape["shard"]
    core = 2 if rep % 2 == 0 else 1
    near = 2 if rep == 16 else 1
    far = rep // (core * near)
    fast = (far, near, core, shard) == (4, 2, 2, 2)
    fine = Mesh(
        np.asarray(mesh.devices).reshape(far, near, core, shard),
        ("far", "near", "core", "shard"),
    )
    every = ("far", "near", "core", "shard")
    row, row3 = P(every, None), P(every, None, None)
    bias, weight = P(None, "shard"), P(None, "shard", None)
    return jax.shard_map(
        local_fast if fast else local_plain,
        mesh=fine,
        in_specs=(
            row3, row, row3, weight, bias, weight, bias, weight, bias, weight, bias, weight, bias,
        ),
        out_specs=(
            row3, row3, row, weight, bias, weight, bias, weight, bias, weight, bias, weight, bias,
        ),
        check_vma=False,
    )
```

time: 995 us -> 760 us (0.76)
  Pallas kernels: 0 us -> 263 us
  starting transfers between devices: 238 us -> 80.2 us
  waiting for transfers between devices: 314 us -> 159 us
  matrix products: 164 us -> 12.7 us
  other arithmetic: 77.5 us -> 53 us
  local copies, waits for them, and re-layouts: 185 us -> 165 us
  between operations: 4.82 us -> 16.8 us
    pallas_call x0 -> x86, Pallas kernels: none -> 263 us  [the longest x58 215 us: call(): pl.pallas_call(kernel, out_shape=[jax.ShapeDtypeStruct(shape, dtype) for...]
    ppermute x57 -> x9, waiting for transfers between devices: 205 us -> 12.6 us  [the longest x6 9.71 us: local_fast(): lax.ppermute(small[l], 'far', [(i, i ^ k) for i in range(4)])]
    unnamed x329 -> x565, local copies, waits for them, and re-layouts: 38.3 us -> 134 us
    ppermute x87 -> x74, starting transfers between devices: 150 us -> 65.1 us  [swap(): return lax.ppermute(value, axis, SWAP)]
    dot_general x30 -> x0, matrix products: 80.8 us -> none  [the longest x18 49 us: t_mm(): lax.dot_general(a, b, (((0,), (0,)), ((), ())), preferred_element_type=f32)]
    ppermute x57 -> x9, starting transfers between devices: 88.2 us -> 14.8 us  [the longest x3 7.59 us: local_fast(): lax.ppermute(silu_all, 'far', [(i, i ^ k) for i in range(4)])]
    psum x0 -> x6, waiting for transfers between devices: none -> 59.5 us  [local_fast(): chain = total[at] = lax.psum(total[at], 'far')]
    dynamic_update_slice x40 -> x0, local copies, waits for them, and re-layouts: 41.1 us -> none  [the longest x32 32.2 us: fetch_rest(): lax.dynamic_update_slice(full, value, (base + (near * 2 + core) * quarter...]
  transfers between devices with their start and end apart: 144 -> 89, of which waited for: 52 -> 19; matrix products, arithmetic and copies ran while one was open for 33% -> 15% of each run, Pallas kernels for 0% -> 24%
where the time goes in v2:
time: 760 us; the launch traced here: 749 us
  Pallas kernels  263 us (35%)
  local copies, waits for them, and re-layouts  165 us (22%)
  waiting for transfers between devices  159 us (21%)
  starting transfers between devices  80.2 us (11%)
  other arithmetic  53 us (7%)
  between operations  16.8 us (2%)
  matrix products  12.7 us (2%)
    pallas_call x58, Pallas kernels, call(): pl.pallas_call(kernel, out_shape=[jax.ShapeDtypeStruct(shape, dtype) for...  215 us
    unnamed x565, local copies, waits for them, and re-layouts  134 us
    ppermute x74, waiting for transfers between devices, swap(): return lax.ppermute(value, axis, SWAP)  86.7 us
    ppermute x74, starting transfers between devices, swap(): return lax.ppermute(value, axis, SWAP)  65.1 us
    psum x6, waiting for transfers between devices, local_fast(): chain = total[at] = lax.psum(total[at], 'far')  59.5 us
    pallas_call x2, Pallas kernels, attention_backward(): pl.pallas_call(kernel, out_shape=jax.ShapeDtypeStruct((tokens, triple), b...  26.6 us
    pallas_call x2, Pallas kernels, attention_forward(): pl.pallas_call(kernel, out_shape=jax.ShapeDtypeStruct((tokens, width), bf...  20.6 us
  transfers between devices with their start and end apart: 89, of which 19 were waited for; matrix products, arithmetic and copies ran while one was open for 15% of the time, Pallas kernels for 24%

profile of v2, /device:TPU:1, one launch (start us, length us, event | category | flops | bytes accessed | tf_op | source)
XLA Modules:
  0.0 749.4 jit_solution(11585545208748108518)
XLA Ops:
  43.2 6.2 collective-permute-done.5.refs_2_
  49.5 5.3 collective-permute-done.3.refs_0_
  58.8 12.6 %collective-permute-done.7.refs_0_ = bf16[384,768]{1,0:T(8,128)(2,1)} collective-permute-done((bf16[384,768]{1,0:T(8,128)(2,1)}, bf16[384,768]{1,0:T(8,128)(2,1)}, u32[]{:S(2)}, u32[]{:S(2)}) %collective-permute-start.7) | collective-permute-done | bytes 589856 | tf_op jit(solution)/shard_map/ppermute | solution.py:70
  90.9 10.3 %shard_map.233.out_ref.lhs_ref = bf16[512,768]{1,0:T(8,128)(2,1)} custom-call(bf16[512,2304]{1,0:T(8,128)(2,1)} %copy-done, bf16[512,2304]{1,0:T(8,128)(2,1)} %copy-done, bf16[512,2304]{1,0:T(8,128)(2,1)} %copy-done), custom_call_target="tpu_custom_call" | custom-call | flops 1 | bytes 1 | tf_op jit(solution)/shard_map/pallas_call | solution.py:397
  117.5 7.2 shard_map.238
  139.0 3.6 collective-permute-start.28
  172.3 10.3 %shard_map.245.out_ref.lhs_ref = bf16[512,768]{1,0:T(8,128)(2,1)} custom-call(bf16[512,2304]{1,0:T(8,128)(2,1)} %copy-done.1, bf16[512,2304]{1,0:T(8,128)(2,1)} %copy-done.1, bf16[512,2304]{1,0:T(8,128)(2,1)} %copy-done.1), custom_call_target="tpu_custom_call" | custom-call | flops 1 | bytes 1 | tf_op jit(solution)/shard_map/pallas_call | solution.py:397
  198.5 7.2 shard_map.250
  209.9 4.3 shard_map.255
  214.5 4.3 collective-permute-done.33.refs_0_
  233.3 8.9 %shard_map.259 = (bf16[512,3072]{1,0:T(8,128)(2,1)S(1)}, f32[2,1,3072]{2,1,0:T(1,128)S(1)}) custom-call(bf16[512,768]{1,0:T(8,128)(2,1)S(1)} %copy-done.40, f32[512,3072]{1,0:T(8,128)} %get-tuple-element.226.pre_ref, bf16[3072,768]{1,0:T(8,128)(2,1)S(1)} %copy-done.21), custom_call_target="tpu_custom_call" | custom-call | flops 1 | bytes 1 | tf_op jit(solution)/shard_map/pallas_call | solution.py:99
  242.8 6.0 shard_map.260
  250.3 3.6 shard_map.253
  253.8 3.6 shard_map.262.refs_2_
  261.2 15.1 %collective-permute-done.35.refs_3_ = bf16[1536,384]{1,0:T(8,128)(2,1)} collective-permute-done((bf16[1536,384]{1,0:T(8,128)(2,1)S(1)}, bf16[1536,384]{1,0:T(8,128)(2,1)}, u32[]{:S(2)}, u32[]{:S(2)}) %collective-permute-start.35) | collective-permute-done | bytes 1179680 | tf_op jit(solution)/shard_map/ppermute | solution.py:70
  282.4 7.9 %shard_map.264 = (f32[512,768]{1,0:T(8,128)S(1)}, bf16[512,768]{1,0:T(8,128)(2,1)S(1)}, bf16[512,768]{1,0:T(8,128)(2,1)S(1)}, f32[2,8,768]{2,1,0:T(8,128)S(1)}) custom-call(bf16[512,3072]{1,0:T(8,128)(2,1)S(1)} %copy-done.3, bf16[768,3072]{1,0:T(8,128)(2,1)} %copy-done.19, bf16[512,768]{1,0:T(8,128)(2,1)S(1)} %bitcast.180, f32[512,768]{1,0:T(8,128)S(1)} %copy-done.175, ...), custom_call_target="tpu_custom_call" | custom-call | flops 1 | bytes 1 | tf_op jit(solution)/shard_map/pallas_call | solution.py:99
  292.6 13.2 %shard_map.265.rhs_ref.grad_ref = bf16[512,2304]{1,0:T(8,128)(2,1)} custom-call(bf16[512,2304]{1,0:T(8,128)(2,1)} %copy-done.1, bf16[512,2304]{1,0:T(8,128)(2,1)} %copy-done.1, bf16[512,2304]{1,0:T(8,128)(2,1)} %copy-done.1, bf16[512,768]{1,0:T(8,128)(2,1)} %copy-done.178), custom_call_target="tpu_custom_call" | custom-call | flops 1 | bytes 1 | tf_op jit(solution)/shard_map/pallas_call | solution.py:435
  308.7 4.7 shard_map.267
  340.4 3.7 shard_map.269.refs_0_
  347.9 4.3 shard_map.275
  363.0 6.1 collective-permute-done.41.refs_2_
  369.0 11.5 %collective-permute-done.42.refs_5_ = bf16[384,1536]{1,0:T(8,128)(2,1)} collective-permute-done((bf16[384,1536]{1,0:T(8,128)(2,1)S(1)}, bf16[384,1536]{1,0:T(8,128)(2,1)}, u32[]{:S(2)}, u32[]{:S(2)}) %collective-permute-start.42) | collective-permute-done | bytes 1179680 | tf_op jit(solution)/shard_map/ppermute | solution.py:70
  384.0 8.8 %shard_map.280 = (bf16[512,3072]{1,0:T(8,128)(2,1)S(1)}, f32[2,1,3072]{2,1,0:T(1,128)S(1)}) custom-call(bf16[512,768]{1,0:T(8,128)(2,1)S(1)} %copy-done.44, f32[512,3072]{1,0:T(8,128)} %get-tuple-element.254.pre_ref, bf16[3072,768]{1,0:T(8,128)(2,1)S(1)} %copy-done.18), custom_call_target="tpu_custom_call" | custom-call | flops 1 | bytes 1 | tf_op jit(solution)/shard_map/pallas_call | solution.py:99
  392.9 5.8 shard_map.281
  413.5 26.0 %all-reduce.7.cloned.1.call-done.refs_1_ = bf16[768,384]{1,0:T(8,128)(2,1)} async-done(((bf16[768,384]{1,0:T(8,128)(2,1)}), bf16[768,384]{1,0:T(8,128)(2,1)}) %all-reduce.7.cloned.1.call-update) | async-done | bytes 589840 | tf_op jit(solution)/shard_map/psum | solution.py:893
  441.3 4.9 shard_map.283.refs_5_
  446.3 4.0 shard_map.282.refs_2_
  459.8 7.8 %shard_map.286 = (f32[512,768]{1,0:T(8,128)S(1)}, bf16[512,768]{1,0:T(8,128)(2,1)S(1)}, bf16[512,768]{1,0:T(8,128)(2,1)S(1)}, f32[2,8,768]{2,1,0:T(8,128)S(1)}) custom-call(bf16[512,3072]{1,0:T(8,128)(2,1)S(1)} %copy-done.11, bf16[768,3072]{1,0:T(8,128)(2,1)} %copy-done.16, f32[512,768]{1,0:T(8,128)S(1)} %copy-done.58, f32[512,768]{1,0:T(8,128)S(1)} %copy-done.169, ...), custom_call_target="tpu_custom_call" | custom-call | flops 1 | bytes 1 | tf_op jit(solution)/shard_map/pallas_call | solution.py:99
  471.1 13.3 %shard_map.287.rhs_ref.grad_ref = bf16[512,2304]{1,0:T(8,128)(2,1)} custom-call(bf16[512,2304]{1,0:T(8,128)(2,1)} %copy-done, bf16[512,2304]{1,0:T(8,128)(2,1)} %copy-done, bf16[512,2304]{1,0:T(8,128)(2,1)} %copy-done, bf16[512,768]{1,0:T(8,128)(2,1)} %copy-done.179), custom_call_target="tpu_custom_call" | custom-call | flops 1 | bytes 1 | tf_op jit(solution)/shard_map/pallas_call | solution.py:435
  489.7 3.6 shard_map.292
  502.5 4.7 shard_map.289
  524.3 3.5 shard_map.294.refs_8_
  527.8 3.5 shard_map.291.refs_3_
  532.7 4.5 collective-permute-done.52.refs_9_
  549.9 7.1 collective-permute-done.54.refs_1_
  569.5 14.4 %collective-permute-done.60.refs_8_ = bf16[192,1536]{1,0:T(8,128)(2,1)S(1)} collective-permute-done((bf16[192,1536]{1,0:T(8,128)(2,1)}, bf16[192,1536]{1,0:T(8,128)(2,1)S(1)}, u32[]{:S(2)}, u32[]{:S(2)}) %collective-permute-start.60) | collective-permute-done | bytes 589856 | tf_op jit(solution)/shard_map/ppermute | solution.py:70
  590.7 3.7 fusion
  595.0 3.8 fusion.18
  614.5 4.7 shard_map.303.refs_0_
  619.2 4.4 shard_map.312.refs_4_
  635.5 12.0 %all-reduce.15.cloned.1.call-done.refs_1_ = bf16[192,1536]{1,0:T(8,128)(2,1)} async-done(((bf16[192,1536]{1,0:T(8,128)(2,1)}), bf16[192,1536]{1,0:T(8,128)(2,1)}) %all-reduce.15.cloned.1.call-update) | async-done | bytes 589840 | tf_op jit(solution)/shard_map/psum | solution.py:893
  655.9 9.2 %shard_map.310.refs_4_ = f32[2,384,3072]{2,1,0:T(8,128)} custom-call(s32[3]{0:T(128)S(1)} %pad_add_fusion.place_ref, bf16[192,1536]{1,0:T(8,128)(2,1)S(1)} %copy-done.127, bf16[192,1536]{1,0:T(8,128)(2,1)} %get-tuple-element.292.refs_1_, bf16[192,1536]{1,0:T(8,128)(2,1)S(1)} %copy-done.141, bf16[192,1536]{1,0:T(8,128)(2,1)} %get-tuple-element.328.refs_3_), custom_call_target="tpu_custom_call" | custom-call | flops 1 | bytes 1 | tf_op jit(solution)/shard_map/pallas_call | solution.py:99
  670.9 5.4 shard_map.306.refs_4_
  676.3 21.5 %all-reduce.17.cloned.1.call-done.refs_5_ = bf16[192,1536]{1,0:T(8,128)(2,1)} async-done(((bf16[192,1536]{1,0:T(8,128)(2,1)}), bf16[192,1536]{1,0:T(8,128)(2,1)}) %all-reduce.17.cloned.1.call-update) | async-done | bytes 589840 | tf_op jit(solution)/shard_map/psum | solution.py:893
  711.4 4.7 collective-permute-done.81.refs_2_
  718.4 4.5 shard_map.304
  727.6 7.0 shard_map.311
  736.9 5.4 shard_map.307
  (934 shorter events, 374.4 us)
Async XLA Ops:
  7.2 432.3 %all-reduce.7.cloned.1.call-start = ((), (), s32[]{:S(2)}) async-start(), calls=%async_computation | async-start | bytes 1179648 | tf_op jit(solution)/shard_map/psum | solution.py:893
  18.3 40.5 %collective-permute-start.11 = (bf16[1,12,128]{2,1,0:T(8,128)(2,1)S(1)}, bf16[1,12,128]{2,1,0:T(8,128)(2,1)S(1)}, u32[]{:S(2)}, u32[]{:S(2)}) collective-permute-start(bf16[1,12,128]{2,1,0:T(8,128)(2,1)S(1)} %reshape.248), channel_id=1, source_target_pairs={{0,2},{2,0},{1,3},{3,1},{4,6},{6,4},{5,7},{7,5},{8,10},{10,8},{9,1... | collective-permute-start | bytes 9224 | tf_op jit(solution)/shard_map/ppermute | solution.py:70
  71.5 35.5 %collective-permute-start.13 = (bf16[384,768]{1,0:T(8,128)(2,1)}, bf16[384,768]{1,0:T(8,128)(2,1)}, u32[]{:S(2)}, u32[]{:S(2)}) collective-permute-start(bf16[384,768]{1,0:T(8,128)(2,1)} %get-tuple-element.180.refs_0_), channel_id=1, source_target_pairs={{0,2},{2,0},{1,3},{3,1},{4,6},{6,4},{5,7},{7,5},{8,10},{10,8},{9,1... | collective-permute-start | bytes 1769480 | tf_op jit(solution)/shard_map/ppermute | solution.py:70
  72.5 34.5 %collective-permute-start.14 = (bf16[384,768]{1,0:T(8,128)(2,1)}, bf16[384,768]{1,0:T(8,128)(2,1)}, u32[]{:S(2)}, u32[]{:S(2)}) collective-permute-start(bf16[384,768]{1,0:T(8,128)(2,1)} %get-tuple-element.180.refs_0_), channel_id=1, source_target_pairs={{0,4},{4,0},{1,5},{5,1},{2,6},{6,2},{3,7},{7,3},{8,12},{12,8},{9,1... | collective-permute-start | bytes 1769480 | tf_op jit(solution)/shard_map/ppermute | solution.py:70
  73.9 33.0 %collective-permute-start.12 = (bf16[96,3072]{1,0:T(8,128)(2,1)}, bf16[96,3072]{1,0:T(8,128)(2,1)S(1)}, u32[]{:S(2)}, u32[]{:S(2)}) collective-permute-start(bf16[96,3072]{1,0:T(8,128)(2,1)} %get-tuple-element.179), channel_id=1, source_target_pairs={{0,1},{1,0},{2,3},{3,2},{4,5},{5,4},{6,7},{7,6},{8,9},{9,8},{10,11... | collective-permute-start | bytes 1769480 | tf_op jit(solution)/shard_map/ppermute | solution.py:70
  75.2 31.8 %collective-permute-start.15 = (bf16[96,3072]{1,0:T(8,128)(2,1)}, bf16[96,3072]{1,0:T(8,128)(2,1)}, u32[]{:S(2)}, u32[]{:S(2)}) collective-permute-start(bf16[96,3072]{1,0:T(8,128)(2,1)} %get-tuple-element.181.refs_1_), channel_id=1, source_target_pairs={{0,2},{2,0},{1,3},{3,1},{4,6},{6,4},{5,7},{7,5},{8,10},{10,8},{9,1... | collective-permute-start | bytes 1769480 | tf_op jit(solution)/shard_map/ppermute | solution.py:70
  77.9 29.0 %collective-permute-start.16 = (bf16[2,12,128]{2,1,0:T(8,128)(2,1)S(1)}, bf16[2,12,128]{2,1,0:T(8,128)(2,1)S(1)}, u32[]{:S(2)}, u32[]{:S(2)}) collective-permute-start(bf16[2,12,128]{2,1,0:T(8,128)(2,1)S(1)} %pad_maximum_fusion.15), channel_id=1, source_target_pairs={{0,1},{1,0},{2,3},{3,2},{4,5},{5,4},{6,7},{7,6},{8,9},{9,8},{10,11... | collective-permute-start | bytes 18440 | tf_op jit(solution)/shard_map/ppermute | solution.py:70
  127.9 26.3 %collective-permute-start.22 = (bf16[384,768]{1,0:T(8,128)(2,1)}, bf16[384,768]{1,0:T(8,128)(2,1)S(1)}, u32[]{:S(2)}, u32[]{:S(2)}) collective-permute-start(bf16[384,768]{1,0:T(8,128)(2,1)} %get-tuple-element.197), channel_id=1, source_target_pairs={{0,1},{1,0},{2,3},{3,2},{4,5},{5,4},{6,7},{7,6},{8,9},{9,8},{10,11... | collective-permute-start | bytes 1769480 | tf_op jit(solution)/shard_map/ppermute | solution.py:70
  128.1 26.1 %collective-permute-start.23 = (bf16[96,3072]{1,0:T(8,128)(2,1)}, bf16[96,3072]{1,0:T(8,128)(2,1)S(1)}, u32[]{:S(2)}, u32[]{:S(2)}) collective-permute-start(bf16[96,3072]{1,0:T(8,128)(2,1)} %get-tuple-element.198.refs_0_), channel_id=1, source_target_pairs={{0,2},{2,0},{1,3},{3,1},{4,6},{6,4},{5,7},{7,5},{8,10},{10,8},{9,1... | collective-permute-start | bytes 1769480 | tf_op jit(solution)/shard_map/ppermute | solution.py:70
  128.6 25.6 %collective-permute-start.24 = (bf16[96,3072]{1,0:T(8,128)(2,1)}, bf16[96,3072]{1,0:T(8,128)(2,1)S(1)}, u32[]{:S(2)}, u32[]{:S(2)}) collective-permute-start(bf16[96,3072]{1,0:T(8,128)(2,1)} %get-tuple-element.198.refs_0_), channel_id=1, source_target_pairs={{0,4},{4,0},{1,5},{5,1},{2,6},{6,2},{3,7},{7,3},{8,12},{12,8},{9,1... | collective-permute-start | bytes 1769480 | tf_op jit(solution)/shard_map/ppermute | solution.py:70
  128.7 25.5 %collective-permute-start.25 = (bf16[96,3072]{1,0:T(8,128)(2,1)}, bf16[96,3072]{1,0:T(8,128)(2,1)S(1)}, u32[]{:S(2)}, u32[]{:S(2)}) collective-permute-start(bf16[96,3072]{1,0:T(8,128)(2,1)} %get-tuple-element.199.refs_1_), channel_id=1, source_target_pairs={{0,2},{2,0},{1,3},{3,1},{4,6},{6,4},{5,7},{7,5},{8,10},{10,8},{9,1... | collective-permute-start | bytes 1769480 | tf_op jit(solution)/shard_map/ppermute | solution.py:70
  156.1 32.2 %collective-permute-start.29 = (bf16[384,768]{1,0:T(8,128)(2,1)}, bf16[384,768]{1,0:T(8,128)(2,1)}, u32[]{:S(2)}, u32[]{:S(2)}) collective-permute-start(bf16[384,768]{1,0:T(8,128)(2,1)} %get-tuple-element.206.refs_0_), channel_id=1, source_target_pairs={{0,2},{2,0},{1,3},{3,1},{4,6},{6,4},{5,7},{7,5},{8,10},{10,8},{9,1... | collective-permute-start | bytes 1769480 | tf_op jit(solution)/shard_map/ppermute | solution.py:70
  158.7 29.6 %collective-permute-start.30 = (bf16[384,768]{1,0:T(8,128)(2,1)}, bf16[384,768]{1,0:T(8,128)(2,1)}, u32[]{:S(2)}, u32[]{:S(2)}) collective-permute-start(bf16[384,768]{1,0:T(8,128)(2,1)} %get-tuple-element.206.refs_0_), channel_id=1, source_target_pairs={{0,4},{4,0},{1,5},{5,1},{2,6},{6,2},{3,7},{7,3},{8,12},{12,8},{9,1... | collective-permute-start | bytes 1769480 | tf_op jit(solution)/shard_map/ppermute | solution.py:70
  159.9 28.4 %collective-permute-start.31 = (bf16[96,3072]{1,0:T(8,128)(2,1)}, bf16[96,3072]{1,0:T(8,128)(2,1)}, u32[]{:S(2)}, u32[]{:S(2)}) collective-permute-start(bf16[96,3072]{1,0:T(8,128)(2,1)} %get-tuple-element.207.refs_1_), channel_id=1, source_target_pairs={{0,2},{2,0},{1,3},{3,1},{4,6},{6,4},{5,7},{7,5},{8,10},{10,8},{9,1... | collective-permute-start | bytes 1769480 | tf_op jit(solution)/shard_map/ppermute | solution.py:70
  188.4 19.0 %collective-permute-start.32 = (bf16[384,768]{1,0:T(8,128)(2,1)}, bf16[384,768]{1,0:T(8,128)(2,1)}, u32[]{:S(2)}, u32[]{:S(2)}) collective-permute-start(bf16[384,768]{1,0:T(8,128)(2,1)} %get-tuple-element.213.refs_1_), channel_id=1, source_target_pairs={{0,2},{2,0},{1,3},{3,1},{4,6},{6,4},{5,7},{7,5},{8,10},{10,8},{9,1... | collective-permute-start | bytes 1769480 | tf_op jit(solution)/shard_map/ppermute | solution.py:70
  249.0 27.3 %collective-permute-start.35 = (bf16[1536,384]{1,0:T(8,128)(2,1)S(1)}, bf16[1536,384]{1,0:T(8,128)(2,1)}, u32[]{:S(2)}, u32[]{:S(2)}) collective-permute-start(bf16[1536,384]{1,0:T(8,128)(2,1)S(1)} %copy-done.130), channel_id=1, source_target_pairs={{0,1},{1,0},{2,3},{3,2},{4,5},{5,4},{6,7},{7,6},{8,9},{9,8},{10,11... | collective-permute-start | bytes 3538952 | tf_op jit(solution)/shard_map/ppermute | solution.py:70
  314.5 30.7 %collective-permute-start.38 = (bf16[384,1536]{1,0:T(8,128)(2,1)}, bf16[384,1536]{1,0:T(8,128)(2,1)}, u32[]{:S(2)}, u32[]{:S(2)}) collective-permute-start(bf16[384,1536]{1,0:T(8,128)(2,1)} %get-tuple-element.242), channel_id=1, source_target_pairs={{0,1},{1,0},{2,3},{3,2},{4,5},{5,4},{6,7},{7,6},{8,9},{9,8},{10,11... | collective-permute-start | bytes 3538952 | tf_op jit(solution)/shard_map/ppermute | solution.py:70
  317.9 27.2 %collective-permute-start.37 = (bf16[768,384]{1,0:T(8,128)(2,1)}, bf16[768,384]{1,0:T(8,128)(2,1)}, u32[]{:S(2)}, u32[]{:S(2)}) collective-permute-start(bf16[768,384]{1,0:T(8,128)(2,1)} %fusion.21), channel_id=1, source_target_pairs={{0,4},{4,0},{1,5},{5,1},{2,6},{6,2},{3,7},{7,3},{8,12},{12,8},{9,1... | collective-permute-start | bytes 1769480 | tf_op jit(solution)/shard_map/ppermute | solution.py:70
  352.8 27.6 %collective-permute-start.42 = (bf16[384,1536]{1,0:T(8,128)(2,1)S(1)}, bf16[384,1536]{1,0:T(8,128)(2,1)}, u32[]{:S(2)}, u32[]{:S(2)}) collective-permute-start(bf16[384,1536]{1,0:T(8,128)(2,1)S(1)} %copy-done.67), channel_id=1, source_target_pairs={{0,1},{1,0},{2,3},{3,2},{4,5},{5,4},{6,7},{7,6},{8,9},{9,8},{10,11... | collective-permute-start | bytes 3538952 | tf_op jit(solution)/shard_map/ppermute | solution.py:70
  398.7 41.5 %collective-permute-start.44 = (bf16[768,1536]{1,0:T(8,128)(2,1)}, bf16[768,1536]{1,0:T(8,128)(2,1)}, u32[]{:S(2)}, u32[]{:S(2)}) collective-permute-start(bf16[768,1536]{1,0:T(8,128)(2,1)} %shard_map.281), channel_id=1, source_target_pairs={{0,2},{2,0},{1,3},{3,1},{4,6},{6,4},{5,7},{7,5},{8,10},{10,8},{9,1... | collective-permute-start | bytes 7077896 | tf_op jit(solution)/shard_map/ppermute | solution.py:70
  404.2 109.2 %all-reduce.9.cloned.1.call-start = ((), (), s32[]{:S(2)}) async-start(), calls=%async_computation.1 | async-start | bytes 1179648 | tf_op jit(solution)/shard_map/psum | solution.py:893
  405.5 45.8 %collective-permute-start.46 = (bf16[1536,384]{1,0:T(8,128)(2,1)}, bf16[1536,384]{1,0:T(8,128)(2,1)}, u32[]{:S(2)}, u32[]{:S(2)}) collective-permute-start(bf16[1536,384]{1,0:T(8,128)(2,1)} %get-tuple-element.258), channel_id=1, source_target_pairs={{0,1},{1,0},{2,3},{3,2},{4,5},{5,4},{6,7},{7,6},{8,9},{9,8},{10,11... | collective-permute-start | bytes 3538952 | tf_op jit(solution)/shard_map/ppermute | solution.py:70
  408.0 43.3 %collective-permute-start.45 = (bf16[192,1536]{1,0:T(8,128)(2,1)}, bf16[192,1536]{1,0:T(8,128)(2,1)}, u32[]{:S(2)}, u32[]{:S(2)}) collective-permute-start(bf16[192,1536]{1,0:T(8,128)(2,1)} %fusion.25), channel_id=1, source_target_pairs={{0,4},{4,0},{1,5},{5,1},{2,6},{6,2},{3,7},{7,3},{8,12},{12,8},{9,1... | collective-permute-start | bytes 1769480 | tf_op jit(solution)/shard_map/ppermute | solution.py:70
  410.0 41.3 %collective-permute-start.43 = (bf16[192,128]{1,0:T(8,128)(2,1)S(1)}, bf16[192,128]{1,0:T(8,128)(2,1)S(1)}, u32[]{:S(2)}, u32[]{:S(2)}) collective-permute-start(bf16[192,128]{1,0:T(8,128)(2,1)S(1)} %pad_maximum_fusion.5), channel_id=1, source_target_pairs={{0,1},{1,0},{2,3},{3,2},{4,5},{5,4},{6,7},{7,6},{8,9},{9,8},{10,11... | collective-permute-start | bytes 147464 | tf_op jit(solution)/shard_map/ppermute | solution.py:70
  440.2 127.9 %all-reduce.11.cloned.1.call-start = ((), (), s32[]{:S(2)}) async-start(), calls=%async_computation.2 | async-start | bytes 1179648 | tf_op jit(solution)/shard_map/psum | solution.py:893
  494.8 37.9 %collective-permute-start.48 = (bf16[768,384]{1,0:T(8,128)(2,1)}, bf16[768,384]{1,0:T(8,128)(2,1)}, u32[]{:S(2)}, u32[]{:S(2)}) collective-permute-start(bf16[768,384]{1,0:T(8,128)(2,1)} %get-tuple-element.260.refs_0_), channel_id=1, source_target_pairs={{0,2},{2,0},{1,3},{3,1},{4,6},{6,4},{5,7},{7,5},{8,10},{10,8},{9,1... | collective-permute-start | bytes 1769480 | tf_op jit(solution)/shard_map/ppermute | solution.py:70
  495.9 36.7 %collective-permute-start.51 = (bf16[768,384]{1,0:T(8,128)(2,1)}, bf16[768,384]{1,0:T(8,128)(2,1)}, u32[]{:S(2)}, u32[]{:S(2)}) collective-permute-start(bf16[768,384]{1,0:T(8,128)(2,1)} %get-tuple-element.260.refs_0_), channel_id=1, source_target_pairs={{0,4},{4,0},{1,5},{5,1},{2,6},{6,2},{3,7},{7,3},{8,12},{12,8},{9,1... | collective-permute-start | bytes 1769480 | tf_op jit(solution)/shard_map/ppermute | solution.py:70
  509.6 23.0 %collective-permute-start.50 = (bf16[768,384]{1,0:T(8,128)(2,1)}, bf16[768,384]{1,0:T(8,128)(2,1)}, u32[]{:S(2)}, u32[]{:S(2)}) collective-permute-start(bf16[768,384]{1,0:T(8,128)(2,1)} %fusion.27), channel_id=1, source_target_pairs={{0,4},{4,0},{1,5},{5,1},{2,6},{6,2},{3,7},{7,3},{8,12},{12,8},{9,1... | collective-permute-start | bytes 1769480 | tf_op jit(solution)/shard_map/ppermute | solution.py:70
  509.9 27.3 %collective-permute-start.52 = (bf16[384,1536]{1,0:T(8,128)(2,1)}, bf16[384,1536]{1,0:T(8,128)(2,1)}, u32[]{:S(2)}, u32[]{:S(2)}) collective-permute-start(bf16[384,1536]{1,0:T(8,128)(2,1)} %get-tuple-element.278), channel_id=1, source_target_pairs={{0,1},{1,0},{2,3},{3,2},{4,5},{5,4},{6,7},{7,6},{8,9},{9,8},{10,11... | collective-permute-start | bytes 3538952 | tf_op jit(solution)/shard_map/ppermute | solution.py:70
  513.5 93.3 %all-reduce.13.cloned.1.call-start = ((), (), s32[]{:S(2)}) async-start(), calls=%async_computation.3 | async-start | bytes 1179648 | tf_op jit(solution)/shard_map/psum | solution.py:893
  537.2 46.7 %collective-permute-start.62 = (bf16[384,1536]{1,0:T(8,128)(2,1)}, bf16[384,1536]{1,0:T(8,128)(2,1)}, u32[]{:S(2)}, u32[]{:S(2)}) collective-permute-start(bf16[384,1536]{1,0:T(8,128)(2,1)} %get-tuple-element.289), channel_id=1, source_target_pairs={{0,1},{1,0},{2,3},{3,2},{4,5},{5,4},{6,7},{7,6},{8,9},{9,8},{10,11... | collective-permute-start | bytes 3538952 | tf_op jit(solution)/shard_map/ppermute | solution.py:70
  549.8 34.1 %collective-permute-start.58 = (bf16[192,1536]{1,0:T(8,128)(2,1)S(1)}, bf16[192,1536]{1,0:T(8,128)(2,1)S(1)}, u32[]{:S(2)}, u32[]{:S(2)}) collective-permute-start(bf16[192,1536]{1,0:T(8,128)(2,1)S(1)} %copy-done.126), channel_id=1, source_target_pairs={{0,2},{2,0},{1,3},{3,1},{4,6},{6,4},{5,7},{7,5},{8,10},{10,8},{9,1... | collective-permute-start | bytes 1769480 | tf_op jit(solution)/shard_map/ppermute | solution.py:70
  557.0 26.9 %collective-permute-start.61 = (bf16[192,1536]{1,0:T(8,128)(2,1)S(1)}, bf16[192,1536]{1,0:T(8,128)(2,1)}, u32[]{:S(2)}, u32[]{:S(2)}) collective-permute-start(bf16[192,1536]{1,0:T(8,128)(2,1)S(1)} %copy-done.126), channel_id=1, source_target_pairs={{0,4},{4,0},{1,5},{5,1},{2,6},{6,2},{3,7},{7,3},{8,12},{12,8},{9,1... | collective-permute-start | bytes 1769480 | tf_op jit(solution)/shard_map/ppermute | solution.py:70
  558.2 25.7 %collective-permute-start.60 = (bf16[192,1536]{1,0:T(8,128)(2,1)}, bf16[192,1536]{1,0:T(8,128)(2,1)S(1)}, u32[]{:S(2)}, u32[]{:S(2)}) collective-permute-start(bf16[192,1536]{1,0:T(8,128)(2,1)} %fusion.29), channel_id=1, source_target_pairs={{0,4},{4,0},{1,5},{5,1},{2,6},{6,2},{3,7},{7,3},{8,12},{12,8},{9,1... | collective-permute-start | bytes 1769480 | tf_op jit(solution)/shard_map/ppermute | solution.py:70
  561.8 22.1 %collective-permute-start.57 = (bf16[768,384]{1,0:T(8,128)(2,1)}, bf16[768,384]{1,0:T(8,128)(2,1)S(1)}, u32[]{:S(2)}, u32[]{:S(2)}) collective-permute-start(bf16[768,384]{1,0:T(8,128)(2,1)} %get-tuple-element.282.refs_1_), channel_id=1, source_target_pairs={{0,2},{2,0},{1,3},{3,1},{4,6},{6,4},{5,7},{7,5},{8,10},{10,8},{9,1... | collective-permute-start | bytes 1769480 | tf_op jit(solution)/shard_map/ppermute | solution.py:70
  568.1 79.4 %all-reduce.15.cloned.1.call-start = ((), (), s32[]{:S(2)}) async-start(), calls=%async_computation.4 | async-start | bytes 1179648 | tf_op jit(solution)/shard_map/psum | solution.py:893
  585.1 41.9 %collective-permute-start.65 = (bf16[192,1536]{1,0:T(8,128)(2,1)}, bf16[192,1536]{1,0:T(8,128)(2,1)S(1)}, u32[]{:S(2)}, u32[]{:S(2)}) collective-permute-start(bf16[192,1536]{1,0:T(8,128)(2,1)} %get-tuple-element.293.refs_0_), channel_id=1, source_target_pairs={{0,2},{2,0},{1,3},{3,1},{4,6},{6,4},{5,7},{7,5},{8,10},{10,8},{9,1... | collective-permute-start | bytes 1769480 | tf_op jit(solution)/shard_map/ppermute | solution.py:70
  586.6 40.4 %collective-permute-start.67 = (bf16[192,1536]{1,0:T(8,128)(2,1)}, bf16[192,1536]{1,0:T(8,128)(2,1)S(1)}, u32[]{:S(2)}, u32[]{:S(2)}) collective-permute-start(bf16[192,1536]{1,0:T(8,128)(2,1)} %get-tuple-element.293.refs_0_), channel_id=1, source_target_pairs={{0,4},{4,0},{1,5},{5,1},{2,6},{6,2},{3,7},{7,3},{8,12},{12,8},{9,1... | collective-permute-start | bytes 1769480 | tf_op jit(solution)/shard_map/ppermute | solution.py:70
  603.4 23.5 %collective-permute-start.66 = (bf16[192,1536]{1,0:T(8,128)(2,1)}, bf16[192,1536]{1,0:T(8,128)(2,1)}, u32[]{:S(2)}, u32[]{:S(2)}) collective-permute-start(bf16[192,1536]{1,0:T(8,128)(2,1)} %fusion.31), channel_id=1, source_target_pairs={{0,4},{4,0},{1,5},{5,1},{2,6},{6,2},{3,7},{7,3},{8,12},{12,8},{9,1... | collective-permute-start | bytes 1769480 | tf_op jit(solution)/shard_map/ppermute | solution.py:70
  603.7 23.3 %collective-permute-start.64 = (bf16[192,1536]{1,0:T(8,128)(2,1)}, bf16[192,1536]{1,0:T(8,128)(2,1)}, u32[]{:S(2)}, u32[]{:S(2)}) collective-permute-start(bf16[192,1536]{1,0:T(8,128)(2,1)} %get-tuple-element.292.refs_1_), channel_id=1, source_target_pairs={{0,2},{2,0},{1,3},{3,1},{4,6},{6,4},{5,7},{7,5},{8,10},{10,8},{9,1... | collective-permute-start | bytes 1769480 | tf_op jit(solution)/shard_map/ppermute | solution.py:70
  606.8 91.0 %all-reduce.17.cloned.1.call-start = ((), (), s32[]{:S(2)}) async-start(), calls=%async_computation.5 | async-start | bytes 1179648 | tf_op jit(solution)/shard_map/psum | solution.py:893
  628.0 19.6 %collective-permute-start.71 = (bf16[768,384]{1,0:T(8,128)(2,1)}, bf16[768,384]{1,0:T(8,128)(2,1)S(1)}, u32[]{:S(2)}, u32[]{:S(2)}) collective-permute-start(bf16[768,384]{1,0:T(8,128)(2,1)} %get-tuple-element.305.refs_0_), channel_id=1, source_target_pairs={{0,2},{2,0},{1,3},{3,1},{4,6},{6,4},{5,7},{7,5},{8,10},{10,8},{9,1... | collective-permute-start | bytes 1769480 | tf_op jit(solution)/shard_map/ppermute | solution.py:70
  628.3 19.3 %collective-permute-start.72 = (bf16[768,384]{1,0:T(8,128)(2,1)}, bf16[768,384]{1,0:T(8,128)(2,1)S(1)}, u32[]{:S(2)}, u32[]{:S(2)}) collective-permute-start(bf16[768,384]{1,0:T(8,128)(2,1)} %get-tuple-element.305.refs_0_), channel_id=1, source_target_pairs={{0,4},{4,0},{1,5},{5,1},{2,6},{6,2},{3,7},{7,3},{8,12},{12,8},{9,1... | collective-permute-start | bytes 1769480 | tf_op jit(solution)/shard_map/ppermute | solution.py:70
  648.8 49.1 %collective-permute-start.77 = (bf16[192,1536]{1,0:T(8,128)(2,1)}, bf16[192,1536]{1,0:T(8,128)(2,1)S(1)}, u32[]{:S(2)}, u32[]{:S(2)}) collective-permute-start(bf16[192,1536]{1,0:T(8,128)(2,1)} %get-tuple-element.311.refs_0_), channel_id=1, source_target_pairs={{0,2},{2,0},{1,3},{3,1},{4,6},{6,4},{5,7},{7,5},{8,10},{10,8},{9,1... | collective-permute-start | bytes 1769480 | tf_op jit(solution)/shard_map/ppermute | solution.py:70
  649.9 48.0 %collective-permute-start.78 = (bf16[192,1536]{1,0:T(8,128)(2,1)}, bf16[192,1536]{1,0:T(8,128)(2,1)S(1)}, u32[]{:S(2)}, u32[]{:S(2)}) collective-permute-start(bf16[192,1536]{1,0:T(8,128)(2,1)} %get-tuple-element.311.refs_0_), channel_id=1, source_target_pairs={{0,4},{4,0},{1,5},{5,1},{2,6},{6,2},{3,7},{7,3},{8,12},{12,8},{9,1... | collective-permute-start | bytes 1769480 | tf_op jit(solution)/shard_map/ppermute | solution.py:70
  651.1 46.7 %collective-permute-start.76 = (bf16[768,384]{1,0:T(8,128)(2,1)}, bf16[768,384]{1,0:T(8,128)(2,1)S(1)}, u32[]{:S(2)}, u32[]{:S(2)}) collective-permute-start(bf16[768,384]{1,0:T(8,128)(2,1)} %get-tuple-element.310.refs_1_), channel_id=1, source_target_pairs={{0,2},{2,0},{1,3},{3,1},{4,6},{6,4},{5,7},{7,5},{8,10},{10,8},{9,1... | collective-permute-start | bytes 1769480 | tf_op jit(solution)/shard_map/ppermute | solution.py:70
  665.2 32.7 %collective-permute-start.74 = (bf16[624,128]{1,0:T(8,128)(2,1)}, bf16[624,128]{1,0:T(8,128)(2,1)S(1)}, u32[]{:S(2)}, u32[]{:S(2)}) collective-permute-start(bf16[624,128]{1,0:T(8,128)(2,1)} %constant_dynamic-update-slice_fusion.23), channel_id=1, source_target_pairs={{0,16},{8,24},{16,0},{24,8},{1,17},{9,25},{17,1},{25,9},{2,18},{10... | collective-permute-start | bytes 479240 | tf_op jit(solution)/shard_map/ppermute | solution.py:910
  666.6 31.3 %collective-permute-start.75 = (bf16[624,128]{1,0:T(8,128)(2,1)}, bf16[624,128]{1,0:T(8,128)(2,1)S(1)}, u32[]{:S(2)}, u32[]{:S(2)}) collective-permute-start(bf16[624,128]{1,0:T(8,128)(2,1)} %constant_dynamic-update-slice_fusion.23), channel_id=1, source_target_pairs={{0,24},{8,16},{16,8},{24,0},{1,25},{9,17},{17,9},{25,1},{2,26},{10... | collective-permute-start | bytes 479240 | tf_op jit(solution)/shard_map/ppermute | solution.py:910
  (308 other events, 1933.0 us)
Sparse Core Ops, SparseCore 0:
  404.3 35.1 all-reduce.6
  441.8 38.7 all-reduce.8
  513.6 43.1 all-reduce.10
  568.2 37.4 all-reduce.12
  608.5 38.9 all-reduce.14
  649.7 48.0 all-reduce.16
